TPU v7x, 256 devices: a whole 4x4x8 slice. The times are simulated.
256 devices in a mesh: seq: 16 (over x_hi, z), head: 16 (over y, x_lo, core).
Axes of the slice: x: 4 (x_hi: 2, x_lo: 2; x = x_hi * 2 + x_lo), y: 4, z: 8, core: 2. Of those that a mesh axis runs over, the one named last changes fastest.
Arguments:
- inputs: bfloat16 [32768, 4096], P('seq', 'head'), may hold values from -6 to 6
- bc_inputs: bfloat16 [32768, 256], P('seq'), may hold values from -6 to 6
- dt_raw: bfloat16 [64, 32768], P(None, 'seq'), may hold values from -2.5 to 2.5
- conv_inner: float32 [4, 4096], replicated, may hold values from -3 to 3
- conv_state: float32 [4, 256], replicated, may hold values from -3 to 3
- log_rate: float32 [64], replicated, may hold values from -2.78 to 1.61
- dt_bias: float32 [64], replicated, as said below
- skip_gain: float32 [64], replicated, may hold values from 0.5 to 2
Outputs:
- mixed: bfloat16 [32768, 4096], P('seq', 'head')
Inputs may be any that keep to these rules, and one draw needn't show every extreme that they name: dt_bias lies between log(4 / 32768) - 0.3 and -4.
All inputs are finite; a program needn't handle non-finite values.
Results may differ from a plain program's by a relative error of at most 0.0034.
Values may be sent and summed in bfloat16 or wider, within the bound.
A program may use at most 128 MiB of HBM per device.

v0:
```python
import jax
import jax.numpy as jnp
from jax import lax
from jax.sharding import PartitionSpec as P

BLOCK = 512


HIGHEST = lax.Precision.HIGHEST


def entering(shard, axis, combine, identity, reverse):
    count, here = (lax.axis_size(axis), lax.axis_index(axis))
    everything = jax.tree.map(lambda part: lax.all_gather(part, axis), shard)
    start = jax.tree.map(
        lambda part, zero: jnp.broadcast_to(jnp.asarray(zero, part.dtype), part.shape),
        shard,
        identity,
    )

    def hop(k, before):
        at = count - 1 - k if reverse else k
        reached = at > here if reverse else at < here
        new = combine(before, jax.tree.map(lambda part: part[at], everything))
        return jax.tree.map(lambda a, b: jnp.where(reached, a, b), new, before)

    return lax.fori_loop(0, count, hop, start)


def partner_2(shard, axis, distance):
    return lax.ppermute(shard, axis, [(i, i ^ 1 << distance) for i in range(lax.axis_size(axis))])


def extended(block, sides, width):
    for axis, dim in sides:
        count = lax.axis_size(axis)
        forward = [(i, i + 1) for i in range(count - 1)]
        backward = [(target, source) for source, target in forward]
        low = lax.ppermute(
            lax.slice_in_dim(block, block.shape[dim] - width, None, axis=dim), axis, forward
        )
        high = lax.ppermute(lax.slice_in_dim(block, 0, width, axis=dim), axis, backward)
        block = jnp.concatenate([low, block, high], axis=dim)
    return block


def causal_taps(padded, weights, row_count, backward):
    tap_count = weights.shape[0]
    total = jnp.zeros((row_count, padded.shape[1]), jnp.float32)
    for tap_index in range(tap_count):
        if backward:
            begin = 2 * (tap_count - 1) - tap_index
        else:
            begin = tap_index
        total = total + weights[tap_index][None, :] * padded[begin : begin + row_count]
    return jax.nn.silu(total)


def block_scan(values, b_part, c_part, steps, rate):
    row_count = values.shape[0]
    head_count = steps.shape[0]
    head_width = values.shape[1] // head_count
    state_size = b_part.shape[1]
    block_count = row_count // BLOCK
    blocked_values = values.reshape(block_count, BLOCK, head_count, head_width)
    blocked_b = b_part.reshape(block_count, BLOCK, state_size)
    blocked_c = c_part.reshape(block_count, BLOCK, state_size)
    blocked_steps = steps.reshape(head_count, block_count, BLOCK).transpose(1, 0, 2)
    lower_mask = jnp.tril(jnp.ones((BLOCK, BLOCK), bool))

    def one_block(carry_pair, block_item):
        carry_state, offset = carry_pair
        value_block, b_block, c_block, step_block = block_item
        cumulative = jnp.cumsum(step_block * rate[:, None], axis=1)
        spread = jnp.where(
            lower_mask[None], cumulative[:, :, None] - cumulative[:, None, :], -jnp.inf
        )
        scores = jnp.dot(c_block, b_block.T, precision=HIGHEST)
        weights = scores[None] * jnp.exp(spread) * step_block[:, None, :]
        inner_part = jnp.einsum("hts,shp->thp", weights, value_block, precision=HIGHEST)
        carried = (
            jnp.einsum("tn,hpn->thp", c_block, carry_state, precision=HIGHEST)
            * jnp.exp(cumulative).T[:, :, None]
        )
        tail_weight = (jnp.exp(cumulative[:, -1:] - cumulative) * step_block).T
        update = jnp.einsum(
            "shp,sn->hpn", value_block * tail_weight[:, :, None], b_block, precision=HIGHEST
        )
        carry_state = jnp.exp(cumulative[:, -1])[:, None, None] * carry_state + update
        return (
            (carry_state, offset + cumulative[:, -1]),
            (inner_part + carried, offset[:, None] + cumulative),
        )

    start_pair = (
        jnp.zeros((head_count, head_width, state_size), jnp.float32),
        jnp.zeros((head_count,), jnp.float32),
    )
    final_pair, stacked = lax.scan(
        one_block, start_pair, (blocked_values, blocked_b, blocked_c, blocked_steps)
    )
    outputs = stacked[0].reshape(row_count, head_count, head_width)
    reach = stacked[1].transpose(1, 0, 2).reshape(head_count, row_count)
    return (outputs, final_pair[0], jnp.exp(final_pair[1]), reach)


def link_states(earlier, later):
    return (earlier[0] * later[0], later[0][:, None, None] * earlier[1] + later[1])


def one_direction(values, b_part, c_part, steps, rate, gain, backward):
    row_count = values.shape[0]
    head_count = steps.shape[0]
    outputs, final_state, total_decay, reach = block_scan(values, b_part, c_part, steps, rate)
    identity = (jnp.ones_like(total_decay), jnp.zeros_like(final_state))
    if backward:
        incoming = entering((total_decay, final_state), "seq", link_states, identity, True)
    else:
        incoming = entering((total_decay, final_state), "seq", link_states, identity, False)
    carried = (
        jnp.einsum("tn,hpn->thp", c_part, incoming[1], precision=HIGHEST)
        * jnp.exp(reach).T[:, :, None]
    )
    shaped = values.reshape(row_count, head_count, -1)
    return outputs + carried + gain[None, :, None] * shaped


def owner_params(owner, conv_inner, log_rate, dt_bias, skip_gain, dt_raw, column_count, head_count):
    weights = lax.dynamic_slice_in_dim(conv_inner, owner * column_count, column_count, 1)
    rate = -jnp.exp(lax.dynamic_slice_in_dim(log_rate, owner * head_count, head_count, 0))
    bias = lax.dynamic_slice_in_dim(dt_bias, owner * head_count, head_count, 0)
    gain = lax.dynamic_slice_in_dim(skip_gain, owner * head_count, head_count, 0)
    raw_steps = lax.dynamic_slice_in_dim(dt_raw, owner * head_count, head_count, 0).astype(
        jnp.float32
    )
    return (weights, rate, bias, gain, raw_steps)


def per_device(inputs, bc_inputs, dt_raw, conv_inner, conv_state, log_rate, dt_bias, skip_gain):
    row_count = inputs.shape[0]
    column_count = inputs.shape[1]
    tap_count = conv_inner.shape[0]
    head_ways = lax.axis_size("head")
    position = lax.axis_index("head")
    head_count = dt_raw.shape[0] // head_ways
    partner = (position + head_ways // 2) % head_ways
    swap_bit = (head_ways // 2).bit_length() - 1
    state_size = bc_inputs.shape[1] // 2
    own_weights, own_rate, own_bias, own_gain, own_raw = owner_params(
        position, conv_inner, log_rate, dt_bias, skip_gain, dt_raw, column_count, head_count
    )
    mate_weights, mate_rate, mate_bias, mate_gain, mate_raw = owner_params(
        partner, conv_inner, log_rate, dt_bias, skip_gain, dt_raw, column_count, head_count
    )
    mate_inputs = partner_2(inputs, "head", swap_bit)
    stacked = jnp.concatenate([inputs, mate_inputs, bc_inputs], axis=1)
    padded = extended(stacked, (("seq", 0),), tap_count - 1).astype(jnp.float32)
    bc_padded = padded[:, padded.shape[1] - 2 * state_size :]
    rev_source = padded[:, column_count : 2 * column_count]
    rev_weights, rev_rate, rev_bias, rev_gain, rev_raw = (
        own_weights,
        own_rate,
        own_bias,
        own_gain,
        mate_raw,
    )
    rev_values = jnp.flip(causal_taps(rev_source, rev_weights, row_count, True), 0)
    rev_bc = jnp.flip(causal_taps(bc_padded, conv_state, row_count, True), 0)
    rev_steps = jnp.flip(jax.nn.softplus(rev_raw + rev_bias[:, None]), 1)
    rev_y = one_direction(
        rev_values,
        rev_bc[:, :state_size],
        rev_bc[:, state_size:],
        rev_steps,
        rev_rate,
        rev_gain,
        True,
    )
    rev_out = jnp.flip(rev_y, 0).reshape(row_count, column_count).astype(jnp.bfloat16)
    fwd_values = causal_taps(padded[:, :column_count], own_weights, row_count, False)
    fwd_bc = causal_taps(bc_padded, conv_state, row_count, False)
    fwd_steps = jax.nn.softplus(own_raw + own_bias[:, None])
    fwd_y = one_direction(
        fwd_values,
        fwd_bc[:, :state_size],
        fwd_bc[:, state_size:],
        fwd_steps,
        own_rate,
        own_gain,
        False,
    )
    fwd_y = fwd_y.reshape(row_count, column_count)
    return (fwd_y + lax.optimization_barrier(rev_out).astype(jnp.float32)).astype(jnp.bfloat16)


def solution(mesh):
    return jax.shard_map(
        per_device,
        mesh=mesh,
        in_specs=(P("seq", "head"), P("seq", None), P(None, "seq"), P(), P(), P(), P(), P()),
        out_specs=P("seq", "head"),
        check_vma=False,
    )
```

profile of v0, /device:TPU:8, one launch (start us, length us, event | category | flops | bytes accessed | tf_op | source)
XLA Modules:
  0.0 500.3 jit_solution(14209147105019219480)
XLA Ops:
  15.4 17.8 %collective-permute-done = bf16[2048,256]{1,0:T(8,128)(2,1)} collective-permute-done((bf16[2048,256]{1,0:T(8,128)(2,1)}, bf16[2048,256]{1,0:T(8,128)(2,1)}, u32[]{:S(2)}, u32[]{:S(2)}) %collective-permute-start) | collective-permute-done | bytes 1048608 | tf_op jit(solution)/shard_map/ppermute | solution.py:31
  41.0 8.1 %rev.13 = f32[4,2048]{1,0:T(4,128)} reverse(f32[4,2048]{1,0:T(4,128)} %get-tuple-element.609), dimensions={1} | reverse | bytes 65536 | tf_op jit(solution)/shard_map/jit(_flip)/rev | solution.py:169
  52.3 15.7 %concatenate.7 = bf16[2054,768]{1,0:T(8,128)(2,1)} concatenate(bf16[3,768]{1,0:T(4,128)(2,1)} %collective-permute-done.1, bf16[2048,768]{1,0:T(8,128)(2,1)S(1)} %constant_dynamic-update-slice_fusion, bf16[3,768]{1,0:T(4,128)(2,1)} %collective-permute-done.2), dimensions={0} | concatenate | bytes 6309888 | tf_op jit(solution)/shard_map/concatenate | solution.py:43
  74.5 13.6 %rev.14 = f32[2048,256]{1,0:T(8,128)S(1)} reverse(f32[2048,256]{1,0:T(8,128)} %get-tuple-element.601), dimensions={0} | reverse | bytes 4194304 | tf_op jit(solution)/shard_map/jit(_flip)/rev | solution.py:167
  96.1 8.1 %divide_multiply_fusion = (f32[2048,256]{1,0:T(8,128)S(1)}, f32[2048,256]{1,0:T(8,128)S(1)}) fusion(f32[2054,768]{1,0:T(8,128)} %copy-done, f32[256]{0:T(256)S(1)} %bitcast.246, f32[256]{0:T(256)S(1)} %bitcast.247, f32[256]{0:T(256)S(1)} %bitcast.245, f32[256]{0:T(256)S(1)} %bitcast.244), kind=kLoop, calls=%fused_computation.148 | loop fusion | flops 11010048 | bytes 18878464 | tf_op jit(solution)/shard_map/jit(silu)/mul | solution.py:56
  106.5 6.8 %slice.172 = f32[2048,128]{1,0:T(8,128)S(1)} reverse(f32[2048,128]{1,0:T(8,128)} %get-tuple-element.605), dimensions={0} | reverse | bytes 2097152 | tf_op jit(solution)/shard_map/slice | solution.py:173
  113.4 8.9 %slice.170 = f32[2048,128]{1,0:T(8,128)} reverse(f32[2048,128]{1,0:T(8,128)} %get-tuple-element.606), dimensions={0} | reverse | bytes 2097152 | tf_op jit(solution)/shard_map/slice | solution.py:172
  123.9 97.1 %while.66 = (s32[]{:T(128)}, f32[4,64,128]{2,1,0:T(8,128)S(1)}, f32[4]{0:T(128)S(1)}, f32[4,512,4,64]{1,0,3,2:T(4,128)}, f32[4,4,512]{2,1,0:T(4,128)S(1)}, /*ind...) while((s32[]{:T(128)}, f32[4,64,128]{2,1,0:T(8,128)S(1)}, ...), condition=%wide.region_9.10_spmd.clone, body=%wide.region_6.9_spmd.clone.sunk | while | flops 1615865856 | bytes 9023225 | solution.py:99
  127.9 6.0 %fusion.170 = f32[512,4,64]{0,2,1:T(8,128)S(1)} fusion(f32[4,512]{1,0:T(4,128)S(1)} %fusion.168, f32[4,512]{1,0:T(4,128)S(1)} %bitcast.230, f32[512,512]{1,0:T(8,128)S(1)} %fusion.169, pred[512,512]{1,0:T(8,128)(4,1)S(1)} %iota_compare_fusion.5, f32[4,512,4,64]{1,3,2,0:T(8,128)} %get-tuple-element.897, s32[]{:T(128)} %get-tuple-element.877), kind=kOutput, calls=%fused_computation.73.clone.1 | convolution fusion | flops 809500672 | bytes 2384384 | tf_op jit(solution)/shard_map/while/body/eval_jaxpr/hts,shp->thp/dot_general | solution.py:80
  135.3 11.1 %dynamic_update_slice.27 = f32[4,512,4,64]{1,0,3,2:T(4,128)} dynamic-update-slice(f32[4,512,4,64]{1,0,3,2:T(4,128)} %get-tuple-element.880, f32[1,512,4,64]{1,0,3,2:T(1,128)S(1)} %copy.82, s32[]{:T(128)} %get-tuple-element.877, s32[]{:T(128)} %constant.138.clone.1..sunk.2, s32[]{:T(128)} %constant.138.clone.1..sunk.2, s32[]{:T(128)} %constant.138.clone.1..sunk.2) | dynamic-update-slice | bytes 1048580 | tf_op jit(solution)/shard_map/while/body/jit(dynamic_update_index_in_dim)/dynamic_update_slice | solution.py:99
  152.1 6.0 %fusion.170 = f32[512,4,64]{0,2,1:T(8,128)S(1)} fusion(f32[4,512]{1,0:T(4,128)S(1)} %fusion.168, f32[4,512]{1,0:T(4,128)S(1)} %bitcast.230, f32[512,512]{1,0:T(8,128)S(1)} %fusion.169, pred[512,512]{1,0:T(8,128)(4,1)S(1)} %iota_compare_fusion.5, f32[4,512,4,64]{1,3,2,0:T(8,128)} %get-tuple-element.897, s32[]{:T(128)} %get-tuple-element.877), kind=kOutput, calls=%fused_computation.73.clone.1 | convolution fusion | flops 809500672 | bytes 2384384 | tf_op jit(solution)/shard_map/while/body/eval_jaxpr/hts,shp->thp/dot_general | solution.py:80
  159.5 11.1 %dynamic_update_slice.27 = f32[4,512,4,64]{1,0,3,2:T(4,128)} dynamic-update-slice(f32[4,512,4,64]{1,0,3,2:T(4,128)} %get-tuple-element.880, f32[1,512,4,64]{1,0,3,2:T(1,128)S(1)} %copy.82, s32[]{:T(128)} %get-tuple-element.877, s32[]{:T(128)} %constant.138.clone.1..sunk.2, s32[]{:T(128)} %constant.138.clone.1..sunk.2, s32[]{:T(128)} %constant.138.clone.1..sunk.2) | dynamic-update-slice | bytes 1048580 | tf_op jit(solution)/shard_map/while/body/jit(dynamic_update_index_in_dim)/dynamic_update_slice | solution.py:99
  176.4 6.0 %fusion.170 = f32[512,4,64]{0,2,1:T(8,128)S(1)} fusion(f32[4,512]{1,0:T(4,128)S(1)} %fusion.168, f32[4,512]{1,0:T(4,128)S(1)} %bitcast.230, f32[512,512]{1,0:T(8,128)S(1)} %fusion.169, pred[512,512]{1,0:T(8,128)(4,1)S(1)} %iota_compare_fusion.5, f32[4,512,4,64]{1,3,2,0:T(8,128)} %get-tuple-element.897, s32[]{:T(128)} %get-tuple-element.877), kind=kOutput, calls=%fused_computation.73.clone.1 | convolution fusion | flops 809500672 | bytes 2384384 | tf_op jit(solution)/shard_map/while/body/eval_jaxpr/hts,shp->thp/dot_general | solution.py:80
  183.7 11.1 %dynamic_update_slice.27 = f32[4,512,4,64]{1,0,3,2:T(4,128)} dynamic-update-slice(f32[4,512,4,64]{1,0,3,2:T(4,128)} %get-tuple-element.880, f32[1,512,4,64]{1,0,3,2:T(1,128)S(1)} %copy.82, s32[]{:T(128)} %get-tuple-element.877, s32[]{:T(128)} %constant.138.clone.1..sunk.2, s32[]{:T(128)} %constant.138.clone.1..sunk.2, s32[]{:T(128)} %constant.138.clone.1..sunk.2) | dynamic-update-slice | bytes 1048580 | tf_op jit(solution)/shard_map/while/body/jit(dynamic_update_index_in_dim)/dynamic_update_slice | solution.py:99
  200.6 6.0 %fusion.170 = f32[512,4,64]{0,2,1:T(8,128)S(1)} fusion(f32[4,512]{1,0:T(4,128)S(1)} %fusion.168, f32[4,512]{1,0:T(4,128)S(1)} %bitcast.230, f32[512,512]{1,0:T(8,128)S(1)} %fusion.169, pred[512,512]{1,0:T(8,128)(4,1)S(1)} %iota_compare_fusion.5, f32[4,512,4,64]{1,3,2,0:T(8,128)} %get-tuple-element.897, s32[]{:T(128)} %get-tuple-element.877), kind=kOutput, calls=%fused_computation.73.clone.1 | convolution fusion | flops 809500672 | bytes 2384384 | tf_op jit(solution)/shard_map/while/body/eval_jaxpr/hts,shp->thp/dot_general | solution.py:80
  208.0 11.1 %dynamic_update_slice.27 = f32[4,512,4,64]{1,0,3,2:T(4,128)} dynamic-update-slice(f32[4,512,4,64]{1,0,3,2:T(4,128)} %get-tuple-element.880, f32[1,512,4,64]{1,0,3,2:T(1,128)S(1)} %copy.82, s32[]{:T(128)} %get-tuple-element.877, s32[]{:T(128)} %constant.138.clone.1..sunk.2, s32[]{:T(128)} %constant.138.clone.1..sunk.2, s32[]{:T(128)} %constant.138.clone.1..sunk.2) | dynamic-update-slice | bytes 1048580 | tf_op jit(solution)/shard_map/while/body/jit(dynamic_update_index_in_dim)/dynamic_update_slice | solution.py:99
  221.0 5.1 %reshape.266 = f32[4,512,4,64]{3,2,1,0:T(4,128)} reshape(f32[2048,256]{1,0:T(8,128)} %get-tuple-element.602) | data formatting | bytes 4194304 | tf_op jit(solution)/shard_map/reshape | solution.py:65
  232.8 97.2 %while.64 = (s32[]{:T(128)}, f32[4,64,128]{2,1,0:T(8,128)S(1)}, f32[4]{0:T(128)S(1)}, f32[4,512,4,64]{1,0,3,2:T(4,128)}, f32[4,4,512]{2,1,0:T(4,128)S(1)}, /*ind...) while((s32[]{:T(128)}, f32[4,64,128]{2,1,0:T(8,128)S(1)}, ...), condition=%wide.region_3.4_spmd.clone, body=%wide.region_0.3_spmd.clone.sunk | while | flops 1615865856 | bytes 9023225 | solution.py:99
  236.8 6.0 %fusion.156 = f32[512,4,64]{0,2,1:T(8,128)S(1)} fusion(f32[4,512]{1,0:T(4,128)S(1)} %fusion.154, f32[4,512]{1,0:T(4,128)S(1)} %bitcast.232, f32[512,512]{1,0:T(8,128)S(1)} %fusion.155, pred[512,512]{1,0:T(8,128)(4,1)S(1)} %iota_compare_fusion.4, f32[4,512,4,64]{1,3,2,0:T(8,128)} %get-tuple-element.858, s32[]{:T(128)} %get-tuple-element.838), kind=kOutput, calls=%fused_computation.20.clone.1 | convolution fusion | flops 809500672 | bytes 2384384 | tf_op jit(solution)/shard_map/while/body/eval_jaxpr/hts,shp->thp/dot_general | solution.py:80
  244.2 11.1 %dynamic_update_slice.25 = f32[4,512,4,64]{1,0,3,2:T(4,128)} dynamic-update-slice(f32[4,512,4,64]{1,0,3,2:T(4,128)} %get-tuple-element.841, f32[1,512,4,64]{1,0,3,2:T(1,128)S(1)} %copy.78, s32[]{:T(128)} %get-tuple-element.838, s32[]{:T(128)} %constant.138.clone.1..sunk, s32[]{:T(128)} %constant.138.clone.1..sunk, s32[]{:T(128)} %constant.138.clone.1..sunk) | dynamic-update-slice | bytes 1048580 | tf_op jit(solution)/shard_map/while/body/jit(dynamic_update_index_in_dim)/dynamic_update_slice | solution.py:99
  261.1 6.0 %fusion.156 = f32[512,4,64]{0,2,1:T(8,128)S(1)} fusion(f32[4,512]{1,0:T(4,128)S(1)} %fusion.154, f32[4,512]{1,0:T(4,128)S(1)} %bitcast.232, f32[512,512]{1,0:T(8,128)S(1)} %fusion.155, pred[512,512]{1,0:T(8,128)(4,1)S(1)} %iota_compare_fusion.4, f32[4,512,4,64]{1,3,2,0:T(8,128)} %get-tuple-element.858, s32[]{:T(128)} %get-tuple-element.838), kind=kOutput, calls=%fused_computation.20.clone.1 | convolution fusion | flops 809500672 | bytes 2384384 | tf_op jit(solution)/shard_map/while/body/eval_jaxpr/hts,shp->thp/dot_general | solution.py:80
  268.5 11.1 %dynamic_update_slice.25 = f32[4,512,4,64]{1,0,3,2:T(4,128)} dynamic-update-slice(f32[4,512,4,64]{1,0,3,2:T(4,128)} %get-tuple-element.841, f32[1,512,4,64]{1,0,3,2:T(1,128)S(1)} %copy.78, s32[]{:T(128)} %get-tuple-element.838, s32[]{:T(128)} %constant.138.clone.1..sunk, s32[]{:T(128)} %constant.138.clone.1..sunk, s32[]{:T(128)} %constant.138.clone.1..sunk) | dynamic-update-slice | bytes 1048580 | tf_op jit(solution)/shard_map/while/body/jit(dynamic_update_index_in_dim)/dynamic_update_slice | solution.py:99
  285.3 6.0 %fusion.156 = f32[512,4,64]{0,2,1:T(8,128)S(1)} fusion(f32[4,512]{1,0:T(4,128)S(1)} %fusion.154, f32[4,512]{1,0:T(4,128)S(1)} %bitcast.232, f32[512,512]{1,0:T(8,128)S(1)} %fusion.155, pred[512,512]{1,0:T(8,128)(4,1)S(1)} %iota_compare_fusion.4, f32[4,512,4,64]{1,3,2,0:T(8,128)} %get-tuple-element.858, s32[]{:T(128)} %get-tuple-element.838), kind=kOutput, calls=%fused_computation.20.clone.1 | convolution fusion | flops 809500672 | bytes 2384384 | tf_op jit(solution)/shard_map/while/body/eval_jaxpr/hts,shp->thp/dot_general | solution.py:80
  292.7 11.1 %dynamic_update_slice.25 = f32[4,512,4,64]{1,0,3,2:T(4,128)} dynamic-update-slice(f32[4,512,4,64]{1,0,3,2:T(4,128)} %get-tuple-element.841, f32[1,512,4,64]{1,0,3,2:T(1,128)S(1)} %copy.78, s32[]{:T(128)} %get-tuple-element.838, s32[]{:T(128)} %constant.138.clone.1..sunk, s32[]{:T(128)} %constant.138.clone.1..sunk, s32[]{:T(128)} %constant.138.clone.1..sunk) | dynamic-update-slice | bytes 1048580 | tf_op jit(solution)/shard_map/while/body/jit(dynamic_update_index_in_dim)/dynamic_update_slice | solution.py:99
  309.6 6.0 %fusion.156 = f32[512,4,64]{0,2,1:T(8,128)S(1)} fusion(f32[4,512]{1,0:T(4,128)S(1)} %fusion.154, f32[4,512]{1,0:T(4,128)S(1)} %bitcast.232, f32[512,512]{1,0:T(8,128)S(1)} %fusion.155, pred[512,512]{1,0:T(8,128)(4,1)S(1)} %iota_compare_fusion.4, f32[4,512,4,64]{1,3,2,0:T(8,128)} %get-tuple-element.858, s32[]{:T(128)} %get-tuple-element.838), kind=kOutput, calls=%fused_computation.20.clone.1 | convolution fusion | flops 809500672 | bytes 2384384 | tf_op jit(solution)/shard_map/while/body/eval_jaxpr/hts,shp->thp/dot_general | solution.py:80
  317.0 11.1 %dynamic_update_slice.25 = f32[4,512,4,64]{1,0,3,2:T(4,128)} dynamic-update-slice(f32[4,512,4,64]{1,0,3,2:T(4,128)} %get-tuple-element.841, f32[1,512,4,64]{1,0,3,2:T(1,128)S(1)} %copy.78, s32[]{:T(128)} %get-tuple-element.838, s32[]{:T(128)} %constant.138.clone.1..sunk, s32[]{:T(128)} %constant.138.clone.1..sunk, s32[]{:T(128)} %constant.138.clone.1..sunk) | dynamic-update-slice | bytes 1048580 | tf_op jit(solution)/shard_map/while/body/jit(dynamic_update_index_in_dim)/dynamic_update_slice | solution.py:99
  335.1 45.7 %all-reduce.2 = (f32[64]{0:T(128)S(1)}, f32[64]{0:T(128)S(1)}) all-reduce(f32[64]{0:T(128)S(1)} %exponential_dynamic-update-slice_fusion.1, f32[64]{0:T(128)S(1)} %exponential_dynamic-update-slice_fusion), channel_id=2, replica_groups=mesh['seq'=16,'head'=16] {'seq'}, use_global_device_ids=true, to_apply=%add | all-reduce | flops 128 | bytes 1024
  388.7 16.8 %while.67 = (s32[]{:T(128)}, f32[4,64,128]{2,1,0:T(8,128)S(1)}, s32[]{:T(128)}, f32[16,4]{1,0:T(8,128)S(1)}, f32[16,4,64,128]{3,2,1,0:T(8,128)}, /*index=5*/s32[]{:T(128)}, s32[]{:T(128)}, s32[]{:T(128)}, s32[]{:T(128)}) while((s32[]{:T(128)}, f32[4,64,128]{2,1,0:T(8,128)S(1)}, s32[]{:T(128)}, f32[16,4]{1,0:T(8,128)S(1)}, ...), condition=%wide.region_11.12_spmd.clone, body=%wide.region_10.11_spmd.clone.sunk | while | flops 131080 | bytes 393431 | solution.py:27
  410.0 7.7 %rev.15 = bf16[2048,4,64]{0,2,1:T(8,128)(2,1)S(1)} reverse(bf16[2048,4,64]{0,2,1:T(8,128)(2,1)} %fusion.89), dimensions={0} | reverse | bytes 2097152 | tf_op jit(solution)/shard_map/jit(_flip)/rev | solution.py:179
  419.0 49.1 %all-gather.7.cloned.1.call-done = f32[64,64,128]{2,1,0:T(8,128)} async-done(((f32[4,64,128]{2,1,0:T(8,128)}), f32[64,64,128]{2,1,0:T(8,128)}) %all-gather.7.cloned.1.call-update) | async-done | bytes 2097168 | tf_op jit(solution)/shard_map/all_gather | solution.py:14
  468.1 16.5 %while.65 = (s32[]{:T(128)}, f32[4,64,128]{2,1,0:T(8,128)S(1)}, s32[]{:T(128)}, f32[16,4]{1,0:T(8,128)S(1)}, f32[16,4,64,128]{3,2,1,0:T(8,128)}, /*index=5*/s32[]{:T(128)}, s32[]{:T(128)}) while((s32[]{:T(128)}, f32[4,64,128]{2,1,0:T(8,128)S(1)}, s32[]{:T(128)}, f32[16,4]{1,0:T(8,128)S(1)}, f32[16,4,64,128]{3,2,1,0:T(8,128)}, ...), condition=%wide.region_5.6_spmd.clone, body=%wide.region_4.5_spmd.clone.sunk | while | flops 131076 | bytes 393369 | solution.py:27
  484.6 5.6 %fusion.91 = f32[2048,4,64]{0,2,1:T(8,128)} fusion(f32[2048,4,64]{0,2,1:T(8,128)} %reshape.235, f32[4,64,128]{2,1,0:T(8,128)S(1)} %get-tuple-element.354, f32[2048,4,64]{0,2,1:T(8,128)} %bitcast.221, f32[4]{0:T(128)S(1)} %copy-done.22, f32[2048,4]{0,1:T(4,128)S(1)} %bitcast.236, f32[2048,256]{1,0:T(8,128)S(1)} %copy-done.6), kind=kOutput, calls=%fused_computation.119 | convolution fusion | flops 807403520 | bytes 7504384 | tf_op jit(solution)/shard_map/tn,hpn->thp/dot_general | solution.py:121
  (333 shorter events, 155.0 us)
Async XLA Ops:
  6.5 382.1 %all-gather.9.cloned.1.call-start = ((), (), s32[]{:S(2)}) async-start(), calls=%async_computation.1 | async-start | bytes 2228224 | tf_op jit(solution)/shard_map/all_gather | solution.py:14
  6.5 26.7 %collective-permute-start = (bf16[2048,256]{1,0:T(8,128)(2,1)}, bf16[2048,256]{1,0:T(8,128)(2,1)}, u32[]{:S(2)}, u32[]{:S(2)}) collective-permute-start(bf16[2048,256]{1,0:T(8,128)(2,1)} %param.16), channel_id=1, source_target_pairs={{0,8},{1,9},{2,10},{3,11},{4,12},{5,13},{6,14},{7,15},{8,0},{9,1},... | collective-permute-start | bytes 3145736 | tf_op jit(solution)/shard_map/ppermute | solution.py:31
  12.5 22.1 %copy-start.10 = (bf16[2048,256]{1,0:T(8,128)(2,1)S(1)}, bf16[2048,256]{1,0:T(8,128)(2,1)}, u32[]{:S(2)}) copy-start(bf16[2048,256]{1,0:T(8,128)(2,1)} %param.17) | copy-start | bytes 3145732
  15.4 25.5 %copy-start.23 = (f32[64]{0:T(128)S(1)}, f32[64]{0:T(128)}, u32[]{:S(2)}) copy-start(f32[64]{0:T(128)} %param.21) | copy-start | bytes 772
  35.2 17.0 %collective-permute-start.1 = (bf16[3,768]{1,0:T(4,128)(2,1)}, bf16[3,768]{1,0:T(4,128)(2,1)}, u32[]{:S(2)}, u32[]{:S(2)}) collective-permute-start(bf16[3,768]{1,0:T(4,128)(2,1)} %get-tuple-element.604), channel_id=1, source_target_pairs={{0,16},{16,32},{32,48},{48,64},{64,80},{80,96},{96,112},{112,128},... | collective-permute-start | bytes 13832 | tf_op jit(solution)/shard_map/ppermute | solution.py:39
  39.6 12.6 %collective-permute-start.2 = (bf16[3,768]{1,0:T(4,128)(2,1)}, bf16[3,768]{1,0:T(4,128)(2,1)}, u32[]{:S(2)}, u32[]{:S(2)}) collective-permute-start(bf16[3,768]{1,0:T(4,128)(2,1)} %get-tuple-element.603), channel_id=1, source_target_pairs={{16,0},{32,16},{48,32},{64,48},{80,64},{96,80},{112,96},{128,112},... | collective-permute-start | bytes 13832 | tf_op jit(solution)/shard_map/ppermute | solution.py:42
  68.0 2.4 copy-start.15
  68.0 2.4 copy-start.16
  68.0 2.4 copy-start.17
  70.4 4.1 copy-start
  88.1 3.2 copy-start.1
  91.3 4.8 copy-start.18
  91.3 4.8 copy-start.19
  91.3 4.8 copy-start.20
  91.3 4.8 copy-start.21
  104.2 2.3 copy-start.5
  113.3 10.6 %copy-start.12 = (f32[4,2048]{1,0:T(4,128)S(1)}, f32[4,2048]{1,0:T(4,128)}, u32[]{:S(2)}) copy-start(f32[4,2048]{1,0:T(4,128)} %rev.13) | copy-start | bytes 98308
  221.0 5.1 %copy-start.4 = (f32[4,64,128]{2,1,0:T(8,128)}, f32[4,64,128]{2,1,0:T(8,128)S(1)}, u32[]{:S(2)}) copy-start(f32[4,64,128]{2,1,0:T(8,128)S(1)} %get-tuple-element.358) | copy-start | bytes 393220
  221.0 5.1 %copy-start.13 = (f32[4,4,512]{2,1,0:T(4,128)}, f32[4,4,512]{2,1,0:T(4,128)S(1)}, u32[]{:S(2)}) copy-start(f32[4,4,512]{2,1,0:T(4,128)S(1)} %get-tuple-element.360) | copy-start | bytes 98308
  231.0 1.8 copy-start.11
  231.0 237.1 %all-gather.7.cloned.1.call-start = ((), (), s32[]{:S(2)}) async-start(), calls=%async_computation | async-start | bytes 2228224 | tf_op jit(solution)/shard_map/all_gather | solution.py:14
  330.0 3.1 copy-start.3
  330.0 3.1 copy-start.2
  380.8 3.7 copy-start.14
  384.6 4.0 copy-start.8
  384.7 20.8 %copy-start.7 = (f32[2048,256]{0,1:T(8,128)S(1)}, f32[2048,256]{0,1:T(8,128)}, u32[]{:S(2)}) copy-start(f32[2048,256]{0,1:T(8,128)} %copy.40) | copy-start | bytes 6291460
  388.6 16.9 %copy-start.22 = (f32[4]{0:T(128)S(1)}, f32[4]{0:T(128)}, u32[]{:S(2)}) copy-start(f32[4]{0:T(128)} %dynamic_slice.83) | copy-start | bytes 52
  417.7 66.9 %copy-start.6 = (f32[2048,256]{1,0:T(8,128)S(1)}, f32[2048,256]{1,0:T(8,128)}, u32[]{:S(2)}) copy-start(f32[2048,256]{1,0:T(8,128)} %copy-done.5) | copy-start | bytes 6291460
  490.3 2.0 copy-start.9
Sparse Core Ops, SparseCore 0:
  231.1 89.6 all-gather.8
  388.8 79.3 all-gather.6
where the time goes:
time: 508 us; the launch traced here: 500 us
  local copies, waits for them, and re-layouts  207 us (41%)
  matrix products  92.4 us (18%)
  waiting for transfers between devices  66.9 us (13%)
  other arithmetic  64.1 us (13%)
  blocking collectives  45.7 us (9%)
  between operations  14.4 us (3%)
  starting transfers between devices  8.02 us (2%)
    dynamic_update_slice x16, local copies, waits for them, and re-layouts, block_scan(): lax.scan(one_block, start_pair, (blocked_values, blocked_b, blocked_c, bl...  93.3 us
    all_gather x2, waiting for transfers between devices, entering(): everything = jax.tree.map(lambda part: lax.all_gather(part, axis), shard)  49.1 us
    dot_general x8, matrix products, one_block(): jnp.einsum('hts,shp->thp', weights, value_block, precision=HIGHEST)  47.9 us
    unnamed x1, blocking collectives  45.7 us
    select_n x32, other arithmetic, hop(): return jax.tree.map(lambda a, b: jnp.where(reached, a, b), new, before)  31.8 us
    ppermute x1, waiting for transfers between devices, partner_2(): lax.ppermute(shard, axis, [(i, i ^ 1 << distance) for i in range(lax.axis...  17.8 us
    rev x2, local copies, waits for them, and re-layouts, per_device(): jnp.flip(causal_taps(rev_source, rev_weights, row_count, True), 0)  16.7 us
    concatenate x1, local copies, waits for them, and re-layouts, extended(): block = jnp.concatenate([low, block, high], axis=dim)  15.7 us
  transfers between devices with their start and end apart: 5, of which 2 were waited for; matrix products, arithmetic and copies ran while one was open for 32% of the time, Pallas kernels for 0%

commit v1 on v0

v1 whole, which is shorter than its diff:
```python
import functools

import jax
import jax.numpy as jnp
from jax import lax
from jax.experimental import pallas as pl
from jax.experimental.pallas import tpu as pltpu
from jax.sharding import PartitionSpec as P

Q = 128
EDGE = 16
HEADS = 4
PIECES = 8
HIGHEST = lax.Precision.HIGHEST
MESH = pl.DeviceIdType.MESH
F32 = jnp.float32
BF16 = jnp.bfloat16


def iota(shape, dim):
    return lax.broadcasted_iota(jnp.int32, shape, dim)


def silu(v):
    h = 0.5 * v
    return h * jnp.tanh(h) + h


def taps(window, weights, begins):
    total = weights[0:1, :] * window[begins[0] : begins[0] + Q]
    for i in range(1, 4):
        total = total + weights[i : i + 1, :] * window[begins[i] : begins[i] + Q]
    return total


def dot(a, b):
    return jnp.dot(a, b, preferred_element_type=F32)


def dot_nt(a, b):
    return lax.dot_general(a, b, (((1,), (1,)), ((), ())), preferred_element_type=F32)


def spread(rows, select):
    high = rows.astype(BF16).astype(F32)
    parts = jnp.concatenate([high, rows - high], axis=0)
    return dot(parts.T.astype(BF16), select)


def kernel(
    seqs, ways,
    x_hbm, bc_hbm, dt_ref, wx_ref, ws_ref, rate_ref, bias_ref, gain_ref,
    out_ref,
    px, pb, pm, gcf, gcr, btr, xsf, xsr, xf, xr, uf, ur, yf, ef, ff, exf, exr,
    run, stot, ra, inc, sin, dmsg, dall,
    local_sem, halo_send, halo_recv, piece_send, piece_recv,
    d_send, d_recv, a_send, a_recv, b_send, b_recv,
):
    rows, width = x_hbm.shape
    chunks = rows // Q
    share = Q // seqs
    here, mine = lax.axis_index("seq"), lax.axis_index("head")
    mate = lax.rem(mine + ways // 2, ways)
    after, before = lax.rem(here + 1, seqs), lax.rem(here + seqs - 1, seqs)

    own_x = pltpu.make_async_copy(x_hbm, px.at[pl.ds(EDGE, rows)], local_sem.at[0])
    own_bc = pltpu.make_async_copy(bc_hbm, pb.at[pl.ds(EDGE, rows)], local_sem.at[1])
    own_x.start()
    own_bc.start()

    barrier = pltpu.get_barrier_semaphore()

    def greet(d, _):
        peer = lax.rem(here + d, seqs)
        pl.semaphore_signal(barrier, inc=1, device_id={"seq": peer, "head": mine}, device_id_type=MESH)
        return 0

    lax.fori_loop(1, seqs, greet, 0)
    for s in (here, after, before):
        pl.semaphore_signal(barrier, inc=1, device_id={"seq": s, "head": mate}, device_id_type=MESH)
    pl.semaphore_wait(barrier, seqs + 2)

    def halo(i, src, dst, s, h):
        return pltpu.make_async_remote_copy(
            src_ref=src, dst_ref=dst, send_sem=halo_send.at[i], recv_sem=halo_recv.at[i],
            device_id={"seq": s, "head": h}, device_id_type=MESH,
        )

    first, last = pl.ds(0, EDGE), pl.ds(rows - EDGE, EDGE)
    low, high = pl.ds(0, EDGE), pl.ds(rows + EDGE, EDGE)
    halos = [
        halo(0, bc_hbm.at[last], pb.at[low], after, mine),
        halo(1, bc_hbm.at[first], pb.at[high], before, mine),
        halo(2, x_hbm.at[last], px.at[low], after, mine),
        halo(3, x_hbm.at[first], pm.at[high], before, mate),
    ]
    for copy in halos:
        copy.start()
    length = rows // PIECES

    def piece(p):
        at = pl.multiple_of(p * length, length)
        return pltpu.make_async_remote_copy(
            src_ref=x_hbm.at[pl.ds(at, length)], dst_ref=pm.at[pl.ds(EDGE + at, length)],
            send_sem=piece_send.at[p], recv_sem=piece_recv.at[p],
            device_id={"seq": here, "head": mate}, device_id_type=MESH,
        )

    def push(i, _):
        piece(PIECES - 1 - i).start()
        return 0

    lax.fori_loop(0, PIECES, push, 0)

    all_heads = dt_ref.shape[0]
    row8, head8 = iota((8, all_heads), 0), iota((8, all_heads), 1)
    owner8 = mine * HEADS + (row8 & (HEADS - 1))
    source8 = owner8 + jnp.where(row8 >= HEADS, all_heads // 2, 0)
    source8 = jnp.where(source8 >= all_heads, source8 - all_heads, source8)
    raw8 = dot((head8 == source8).astype(F32).astype(BF16), dt_ref[...])
    chosen = head8 == owner8

    def pick(values):
        return jnp.sum(jnp.where(chosen, values, 0.0), axis=1, keepdims=True)

    rate8 = pick(-jnp.exp(rate_ref[...]))
    gain8 = pick(gain_ref[...])
    pre = raw8 + pick(bias_ref[...])
    dt8 = jnp.maximum(pre, 0.0) + jnp.log1p(jnp.exp(-jnp.abs(pre)))
    dt = jnp.concatenate([dt8[:, k * Q : (k + 1) * Q] for k in range(chunks)], axis=0)
    logs8 = dt8 * rate8
    logs = jnp.concatenate([logs8[:, k * Q : (k + 1) * Q] for k in range(chunks)], axis=0)
    r, c = iota((Q, Q), 0), iota((Q, Q), 1)
    upto = jnp.dot(logs, (r <= c).astype(F32), precision=HIGHEST, preferred_element_type=F32)
    onward = jnp.dot(logs, (r >= c).astype(F32), precision=HIGHEST, preferred_element_type=F32)
    is_forward = (iota((chunks * 8, Q), 0) & 7) < HEADS
    cum = jnp.where(is_forward, upto, onward)
    half = 0.5 * jnp.sum(logs, axis=1, keepdims=True)
    ef[...] = jnp.exp(cum - half)
    ff[...] = dt * jnp.exp(half - cum)
    per = width // HEADS
    head_row, head_col = iota((chunks * 8, width), 0) & 7, iota((chunks * 8, width), 1) // per
    to_chunk = (iota((chunks, chunks * 8), 1) // 8 == iota((chunks, chunks * 8), 0)).astype(F32)
    totals = []
    for offset, where in ((0, exf), (HEADS, exr)):
        wide = jnp.where(head_row == head_col + offset, half, 0.0)
        summed = jnp.dot(to_chunk, wide, precision=HIGHEST, preferred_element_type=F32)
        where[...] = jnp.exp(summed)
        totals.append(jnp.exp(2.0 * jnp.sum(summed, axis=0, keepdims=True)))
    gain = jnp.sum(
        jnp.where(iota((8, width), 0) == iota((8, width), 1) // per, gain8, 0.0), axis=0, keepdims=True
    )
    sel_row, sel_col = iota((16, width), 0) & 7, iota((16, width), 1) // per
    select_f = (sel_row == sel_col).astype(F32).astype(BF16)
    select_r = (sel_row == sel_col + HEADS).astype(F32).astype(BF16)
    decay = jnp.where(iota((8, width), 0) == 0, totals[0], totals[1])
    dmsg[...] = decay
    dall[here] = decay

    def tell(d):
        return pltpu.make_async_remote_copy(
            src_ref=dmsg, dst_ref=dall.at[here], send_sem=d_send.at[d], recv_sem=d_recv.at[d],
            device_id={"seq": lax.rem(here + d, seqs), "head": mine}, device_id_type=MESH,
        )

    def tell_start(d, _):
        tell(d).start()
        return 0

    lax.fori_loop(1, seqs, tell_start, 0)

    weights_x = wx_ref[:, pl.ds(pl.multiple_of(mine * width, width), width)]
    weights_s = ws_ref[...]

    own_x.wait()
    own_bc.wait()
    for i in range(3):
        halos[i].wait_recv()

    @pl.when(here == 0)
    def _():
        px[pl.ds(0, EDGE), :] = jnp.zeros((EDGE, width), BF16)
        pb[pl.ds(0, EDGE), :] = jnp.zeros((EDGE, width), BF16)

    @pl.when(here == seqs - 1)
    def _():
        pb[pl.ds(rows + EDGE, EDGE), :] = jnp.zeros((EDGE, width), BF16)

    def step_forward(k, state):
        at = pl.multiple_of(k * Q, Q)
        window = pb[pl.ds(at, Q + 2 * EDGE), :].astype(F32)
        fwd = silu(taps(window, weights_s, [EDGE - 3, EDGE - 2, EDGE - 1, EDGE]))
        rev = silu(taps(window, weights_s, [EDGE + 3, EDGE + 2, EDGE + 1, EDGE]))
        bf, cf = fwd[:, :Q].astype(BF16), fwd[:, Q:].astype(BF16)
        br, cr = rev[:, :Q].astype(BF16), rev[:, Q:].astype(BF16)
        gcf[pl.ds(at, Q), Q:] = cf
        gcr[pl.ds(at, Q), Q:] = cr
        gcf[pl.ds(at, Q), :Q] = jnp.where(r >= c, dot_nt(cf, bf), 0.0).astype(BF16)
        gcr[pl.ds(at, Q), :Q] = jnp.where(r <= c, dot_nt(cr, br), 0.0).astype(BF16)
        btr[pl.ds(at, Q), :] = rev[:, :Q].T.astype(BF16)
        window = px[pl.ds(at, Q + EDGE), :].astype(F32)
        value = silu(taps(window, weights_x, [EDGE - 3, EDGE - 2, EDGE - 1, EDGE]))
        xf[pl.ds(at, Q), :] = value
        scaled = (value * spread(ff[pl.ds(pl.multiple_of(k * 8, 8), 8), :], select_f)).astype(BF16)
        xsf[k, :Q, :] = scaled
        update = dot(fwd[:, :Q].T.astype(BF16), scaled)
        uf[k] = update
        e = exf[pl.ds(k, 1), :]
        return e * (e * state + update)

    stot[0] = lax.fori_loop(0, chunks, step_forward, jnp.zeros((Q, width), F32))

    def to_owner(way, d):
        peer = lax.rem(here + d, seqs)
        return pltpu.make_async_remote_copy(
            src_ref=stot.at[way, pl.ds(pl.multiple_of(peer * share, share), share)],
            dst_ref=ra.at[way, here], send_sem=a_send.at[way, d], recv_sem=a_recv.at[way, d],
            device_id={"seq": peer, "head": mine}, device_id_type=MESH,
        )

    def from_owner(way, d):
        peer = lax.rem(here + d, seqs)
        return pltpu.make_async_remote_copy(
            src_ref=inc.at[way, peer],
            dst_ref=sin.at[way, pl.ds(pl.multiple_of(here * share, share), share)],
            send_sem=b_send.at[way, d], recv_sem=b_recv.at[way, d],
            device_id={"seq": peer, "head": mine}, device_id_type=MESH,
        )

    mine_rows = pl.ds(pl.multiple_of(here * share, share), share)

    def states_out(way):
        def go(d, _):
            to_owner(way, d).start()
            return 0

        lax.fori_loop(1, seqs, go, 0)
        ra[way, here] = stot[way, mine_rows, :]

    def states_back(way):
        def arrive(d, _):
            to_owner(way, d).wait_recv()
            return 0

        lax.fori_loop(1, seqs, arrive, 0)

        def hop(i, entering):
            at = i if way == 0 else seqs - 1 - i
            inc[way, at] = entering
            return dall[at, way : way + 1, :] * entering + ra[way, at]

        lax.fori_loop(0, seqs, hop, jnp.zeros((share, width), F32))

        def go(d, _):
            from_owner(way, d).start()
            return 0

        lax.fori_loop(1, seqs, go, 0)
        sin[way, mine_rows, :] = inc[way, here]

    def states_in(way):
        def arrive(d, _):
            from_owner(way, d).wait_recv()
            return 0

        lax.fori_loop(1, seqs, arrive, 0)

    def step_reverse(k):
        at = pl.multiple_of(k * Q, Q)
        window = pm[pl.ds(EDGE + at, Q + EDGE), :].astype(F32)
        value = silu(taps(window, weights_x, [3, 2, 1, 0]))
        xr[pl.ds(at, Q), :] = value
        scaled = (value * spread(ff[pl.ds(pl.multiple_of(k * 8, 8), 8), :], select_r)).astype(BF16)
        xsr[k, :Q, :] = scaled
        update = dot(btr[pl.ds(at, Q), :], scaled)
        ur[k] = update
        e = exr[pl.ds(k, 1), :]
        run[...] = e * (e * run[...] + update)

    each = chunks // PIECES

    def pieces(start, stop):
        def one(i, _):
            p = PIECES - 1 - i
            piece(p).wait_recv()

            def inner(j, _):
                step_reverse(p * each + each - 1 - j)
                return 0

            lax.fori_loop(0, each, inner, 0)
            return 0

        lax.fori_loop(start, stop, one, 0)

    states_out(0)
    run[...] = jnp.zeros((Q, width), F32)
    halos[3].wait_recv()

    @pl.when(here == seqs - 1)
    def _():
        pm[pl.ds(rows + EDGE, EDGE), :] = jnp.zeros((EDGE, width), BF16)

    pieces(0, 2)

    def told(d, _):
        tell(d).wait_recv()
        return 0

    lax.fori_loop(1, seqs, told, 0)
    states_back(0)
    pieces(2, 4)
    states_in(0)

    def finish_forward(k, state):
        at = pl.multiple_of(k * Q, Q)
        e = exf[pl.ds(k, 1), :]
        entering = e * state
        xsf[k, Q:, :] = entering.astype(BF16)
        y = dot(gcf[pl.ds(at, Q), :], xsf[k])
        scale = spread(ef[pl.ds(pl.multiple_of(k * 8, 8), 8), :], select_f)
        yf[pl.ds(at, Q), :] = scale * y + gain * xf[pl.ds(at, Q), :]
        return e * (entering + uf[k])

    lax.fori_loop(0, chunks, finish_forward, sin[0])
    pieces(4, PIECES)
    stot[1] = run[...]
    states_out(1)
    states_back(1)
    states_in(1)

    def finish_reverse(i, state):
        k = chunks - 1 - i
        at = pl.multiple_of(k * Q, Q)
        e = exr[pl.ds(k, 1), :]
        entering = e * state
        xsr[k, Q:, :] = entering.astype(BF16)
        y = dot(gcr[pl.ds(at, Q), :], xsr[k])
        scale = spread(ef[pl.ds(pl.multiple_of(k * 8, 8), 8), :], select_r)
        back = (scale * y + gain * xr[pl.ds(at, Q), :]).astype(BF16)
        out_ref[pl.ds(at, Q), :] = (yf[pl.ds(at, Q), :] + back.astype(F32)).astype(BF16)
        return e * (entering + ur[k])

    lax.fori_loop(0, chunks, finish_reverse, sin[1])

    for copy in halos:
        copy.wait_send()

    def sent_piece(p, _):
        piece(p).wait_send()
        return 0

    lax.fori_loop(0, PIECES, sent_piece, 0)

    def sent(d, _):
        tell(d).wait_send()
        for way in (0, 1):
            to_owner(way, d).wait_send()
            from_owner(way, d).wait_send()
        return 0

    lax.fori_loop(1, seqs, sent, 0)


def per_device(inputs, bc_inputs, dt_raw, conv_inner, conv_state, log_rate, dt_bias, skip_gain):
    seqs, ways = lax.axis_size("seq"), lax.axis_size("head")
    rows, width = inputs.shape
    chunks, share = rows // Q, Q // seqs
    anywhere = pl.BlockSpec(memory_space=pl.ANY)
    vmem = pl.BlockSpec(memory_space=pltpu.VMEM)
    padded = pltpu.VMEM((rows + 2 * EDGE, width), BF16)
    dma = pltpu.SemaphoreType.DMA
    return pl.pallas_call(
        functools.partial(kernel, seqs, ways),
        out_shape=jax.ShapeDtypeStruct((rows, width), BF16),
        in_specs=[anywhere, anywhere] + [vmem] * 6,
        out_specs=vmem,
        scratch_shapes=[
            padded, padded, padded,
            pltpu.VMEM((rows, 2 * Q), BF16), pltpu.VMEM((rows, 2 * Q), BF16), pltpu.VMEM((rows, Q), BF16),
            pltpu.VMEM((chunks, 2 * Q, width), BF16), pltpu.VMEM((chunks, 2 * Q, width), BF16),
            pltpu.VMEM((rows, width), F32), pltpu.VMEM((rows, width), F32),
            pltpu.VMEM((chunks, Q, width), F32), pltpu.VMEM((chunks, Q, width), F32),
            pltpu.VMEM((rows, width), F32),
            pltpu.VMEM((chunks * 8, Q), F32), pltpu.VMEM((chunks * 8, Q), F32),
            pltpu.VMEM((chunks, width), F32), pltpu.VMEM((chunks, width), F32),
            pltpu.VMEM((Q, width), F32), pltpu.VMEM((2, Q, width), F32),
            pltpu.VMEM((2, seqs, share, width), F32), pltpu.VMEM((2, seqs, share, width), F32),
            pltpu.VMEM((2, Q, width), F32),
            pltpu.VMEM((8, width), F32), pltpu.VMEM((seqs, 8, width), F32),
            dma((2,)), dma((4,)), dma((4,)), dma((PIECES,)), dma((PIECES,)),
            dma((seqs,)), dma((seqs,)), dma((2, seqs)), dma((2, seqs)), dma((2, seqs)), dma((2, seqs)),
        ],
        compiler_params=pltpu.CompilerParams(
            collective_id=0, has_side_effects=True, vmem_limit_bytes=48 * 2**20
        ),
    )(
        inputs, bc_inputs, dt_raw, conv_inner, conv_state,
        log_rate[None, :], dt_bias[None, :], skip_gain[None, :],
    )


def solution(mesh):
    return jax.shard_map(
        per_device,
        mesh=mesh,
        in_specs=(P("seq", "head"), P("seq", None), P(None, "seq"), P(), P(), P(), P(), P()),
        out_specs=P("seq", "head"),
        check_vma=False,
    )
```

time: 508 us -> 67.7 us (0.13); the launches traced: 500 us -> 67.4 us
  local copies, waits for them, and re-layouts: 207 us -> 5.9 us
  matrix products: 92.4 us -> 0 us
  waiting for transfers between devices: 66.9 us -> 0 us
  other arithmetic: 64.1 us -> 0 us
  Pallas kernels: 0 us -> 61.5 us
  blocking collectives: 45.7 us -> 0 us
  between operations: 14.4 us -> 0.03 us
  starting transfers between devices: 8.02 us -> 0 us
    dynamic_update_slice x16 -> x0, local copies, waits for them, and re-layouts: 93.3 us -> none  [block_scan(): lax.scan(one_block, start_pair, (blocked_values, blocked_b, blocked_c, bl...]
    dot_general x34 -> x0, matrix products: 92.4 us -> none  [the longest x8 47.9 us: one_block(): jnp.einsum('hts,shp->thp', weights, value_block, precision=HIGHEST)]
    pallas_call x0 -> x1, Pallas kernels: none -> 61.5 us  [per_device(): pl.pallas_call(functools.partial(kernel, seqs, ways), out_shape=jax.Shape...]
    all_gather x2 -> x0, waiting for transfers between devices: 49.1 us -> none  [entering(): everything = jax.tree.map(lambda part: lax.all_gather(part, axis), shard)]
    unnamed x1 -> x0, blocking collectives: 45.7 us -> none
    select_n x33 -> x0, other arithmetic: 33.4 us -> none  [the longest x32 31.8 us: hop(): return jax.tree.map(lambda a, b: jnp.where(reached, a, b), new, before)]
    rev x4 -> x0, local copies, waits for them, and re-layouts: 32.5 us -> none  [the longest x2 16.7 us: per_device(): jnp.flip(causal_taps(rev_source, rev_weights, row_count, True), 0)]
    slice x18 -> x0, local copies, waits for them, and re-layouts: 22.2 us -> none  [the longest x1 8.87 us: per_device(): rev_bc[:, :state_size]]
  transfers between devices with their start and end apart: 5 -> 0, of which waited for: 2 -> 0; matrix products, arithmetic and copies ran while one was open for 32% -> 0% of each run, Pallas kernels for 0% -> 0%
where the time goes in v1:
time: 67.7 us; the launch traced here: 67.4 us
  Pallas kernels  61.5 us (91%)
  local copies, waits for them, and re-layouts  5.9 us (9%)
    pallas_call x1, Pallas kernels, per_device(): pl.pallas_call(functools.partial(kernel, seqs, ways), out_shape=jax.Shape...  61.5 us
    unnamed x17, local copies, waits for them, and re-layouts  5.9 us

profile of v1, /device:TPU:8, one launch (start us, length us, event | category | flops | bytes accessed | tf_op | source)
XLA Modules:
  0.0 67.4 jit_solution(16351240198222469173)
XLA Ops:
  0.0 0.0 copy-start.4
  0.0 0.0 copy-start.5
  0.0 0.0 copy-start.6
  0.0 0.0 copy-start.7
  0.0 0.7 copy-done.4
  0.7 0.0 copy-done.5
  0.7 0.0 copy-done.6
  0.7 0.0 copy-done.7
  0.7 0.0 copy-start
  0.7 1.2 %copy-done = bf16[2048,256]{1,0:T(8,128)(2,1)S(1)} copy-done((bf16[2048,256]{1,0:T(8,128)(2,1)S(1)}, bf16[2048,256]{1,0:T(8,128)(2,1)}, u32[]{:S(2)}) %copy-start) | copy-done | bytes 1048600
  1.9 0.0 copy-start.1
  1.9 1.2 %copy-done.1 = bf16[2048,256]{1,0:T(8,128)(2,1)S(1)} copy-done((bf16[2048,256]{1,0:T(8,128)(2,1)S(1)}, bf16[2048,256]{1,0:T(8,128)(2,1)}, u32[]{:S(2)}) %copy-start.1) | copy-done | bytes 1048600
  3.2 0.0 copy-start.2
  3.2 0.9 %copy-done.2 = bf16[64,2048]{1,0:T(8,128)(2,1)S(1)} copy-done((bf16[64,2048]{1,0:T(8,128)(2,1)S(1)}, bf16[64,2048]{1,0:T(8,128)(2,1)}, u32[]{:S(2)}) %copy-start.2) | copy-done | bytes 262168
  4.1 0.0 copy-start.3
  4.1 0.8 %copy-done.3 = f32[4,4096]{1,0:T(4,128)S(1)} copy-done((f32[4,4096]{1,0:T(4,128)S(1)}, f32[4,4096]{1,0:T(4,128)}, u32[]{:S(2)}) %copy-start.3) | copy-done | bytes 65560
  4.9 61.5 %shard_map.82 = bf16[2048,256]{1,0:T(8,128)(2,1)S(1)} custom-call(bf16[2048,256]{1,0:T(8,128)(2,1)S(1)} %copy-done, bf16[2048,256]{1,0:T(8,128)(2,1)S(1)} %copy-done.1, bf16[64,2048]{1,0:T(8,128)(2,1)S(1)} %copy-done.2, f32[4,4096]{1,0:T(4,128)S(1)} %copy-done.3, f32[4,256]{1,0:T(4,128)S(1)} %copy-done.4, f32[1,64]{1,0:T(1,128)S(1)} %bitcast.3, ...), custom_call_target="tpu_custom_call" | custom-call | tf_op jit(solution)/shard_map/pallas_call | solution.py:373
  66.5 1.0 %copy.10 = bf16[2048,256]{1,0:T(8,128)(2,1)} copy(bf16[2048,256]{1,0:T(8,128)(2,1)S(1)} %shard_map.82) | data formatting | bytes 2097152
Async XLA Ops:
  0.0 0.7 %copy-start.4 = (f32[4,256]{1,0:T(4,128)S(1)}, f32[4,256]{1,0:T(4,128)}, u32[]{:S(2)}) copy-start(f32[4,256]{1,0:T(4,128)} %ws_ref.1) | copy-start | bytes 12292
  0.0 0.7 %copy-start.5 = (f32[64]{0:T(128)S(1)}, f32[64]{0:T(128)}, u32[]{:S(2)}) copy-start(f32[64]{0:T(128)} %param.13) | copy-start | bytes 772
  0.0 0.7 %copy-start.6 = (f32[64]{0:T(128)S(1)}, f32[64]{0:T(128)}, u32[]{:S(2)}) copy-start(f32[64]{0:T(128)} %param.14) | copy-start | bytes 772
  0.0 0.7 %copy-start.7 = (f32[64]{0:T(128)S(1)}, f32[64]{0:T(128)}, u32[]{:S(2)}) copy-start(f32[64]{0:T(128)} %param.15) | copy-start | bytes 772
  0.7 1.2 %copy-start = (bf16[2048,256]{1,0:T(8,128)(2,1)S(1)}, bf16[2048,256]{1,0:T(8,128)(2,1)}, u32[]{:S(2)}) copy-start(bf16[2048,256]{1,0:T(8,128)(2,1)} %x_hbm.1) | copy-start | bytes 3145732
  1.9 1.2 %copy-start.1 = (bf16[2048,256]{1,0:T(8,128)(2,1)S(1)}, bf16[2048,256]{1,0:T(8,128)(2,1)}, u32[]{:S(2)}) copy-start(bf16[2048,256]{1,0:T(8,128)(2,1)} %bc_hbm.1) | copy-start | bytes 3145732
  3.2 0.9 %copy-start.2 = (bf16[64,2048]{1,0:T(8,128)(2,1)S(1)}, bf16[64,2048]{1,0:T(8,128)(2,1)}, u32[]{:S(2)}) copy-start(bf16[64,2048]{1,0:T(8,128)(2,1)} %dt_ref.1) | copy-start | bytes 786436
  4.1 0.8 %copy-start.3 = (f32[4,4096]{1,0:T(4,128)S(1)}, f32[4,4096]{1,0:T(4,128)}, u32[]{:S(2)}) copy-start(f32[4,4096]{1,0:T(4,128)} %wx_ref.1) | copy-start | bytes 196612

commit v2 on v1

--- a/solution.py
+++ b/solution.py
@@ -49,9 +49,9 @@
 
 def kernel(
     seqs, ways,
-    x_hbm, bc_hbm, dt_ref, wx_ref, ws_ref, rate_ref, bias_ref, gain_ref,
+    x_hbm, bc_hbm, dt_hbm, wx_hbm, ws_ref, rate_ref, bias_ref, gain_ref,
     out_ref,
-    px, pb, pm, gcf, gcr, btr, xsf, xsr, xf, xr, uf, ur, yf, ef, ff, exf, exr,
+    dt_ref, wx_ref, px, pb, pm, gcf, gcr, btr, xsf, xsr, xf, xr, uf, ur, yf, ef, ff, exf, exr,
     run, stot, ra, inc, sin, dmsg, dall,
     local_sem, halo_send, halo_recv, piece_send, piece_recv,
     d_send, d_recv, a_send, a_recv, b_send, b_recv,
@@ -60,57 +60,30 @@
     chunks = rows // Q
     share = Q // seqs
     here, mine = lax.axis_index("seq"), lax.axis_index("head")
-    mate = lax.rem(mine + ways // 2, ways)
-    after, before = lax.rem(here + 1, seqs), lax.rem(here + seqs - 1, seqs)
+    mate = (mine + ways // 2) & (ways - 1)
+    after, before = (here + 1) & (seqs - 1), (here - 1) & (seqs - 1)
 
     own_x = pltpu.make_async_copy(x_hbm, px.at[pl.ds(EDGE, rows)], local_sem.at[0])
     own_bc = pltpu.make_async_copy(bc_hbm, pb.at[pl.ds(EDGE, rows)], local_sem.at[1])
-    own_x.start()
-    own_bc.start()
+    own_dt = pltpu.make_async_copy(dt_hbm, dt_ref, local_sem.at[2])
+    columns = pl.ds(pl.multiple_of(mine * width, width), width)
+    own_w = pltpu.make_async_copy(wx_hbm.at[:, columns], wx_ref, local_sem.at[3])
 
     barrier = pltpu.get_barrier_semaphore()
 
     def greet(d, _):
-        peer = lax.rem(here + d, seqs)
+        peer = (here + d) & (seqs - 1)
         pl.semaphore_signal(barrier, inc=1, device_id={"seq": peer, "head": mine}, device_id_type=MESH)
         return 0
 
     lax.fori_loop(1, seqs, greet, 0)
     for s in (here, after, before):
         pl.semaphore_signal(barrier, inc=1, device_id={"seq": s, "head": mate}, device_id_type=MESH)
-    pl.semaphore_wait(barrier, seqs + 2)
-
-    def halo(i, src, dst, s, h):
-        return pltpu.make_async_remote_copy(
-            src_ref=src, dst_ref=dst, send_sem=halo_send.at[i], recv_sem=halo_recv.at[i],
-            device_id={"seq": s, "head": h}, device_id_type=MESH,
-        )
-
-    first, last = pl.ds(0, EDGE), pl.ds(rows - EDGE, EDGE)
-    low, high = pl.ds(0, EDGE), pl.ds(rows + EDGE, EDGE)
-    halos = [
-        halo(0, bc_hbm.at[last], pb.at[low], after, mine),
-        halo(1, bc_hbm.at[first], pb.at[high], before, mine),
-        halo(2, x_hbm.at[last], px.at[low], after, mine),
-        halo(3, x_hbm.at[first], pm.at[high], before, mate),
-    ]
-    for copy in halos:
-        copy.start()
-    length = rows // PIECES
-
-    def piece(p):
-        at = pl.multiple_of(p * length, length)
-        return pltpu.make_async_remote_copy(
-            src_ref=x_hbm.at[pl.ds(at, length)], dst_ref=pm.at[pl.ds(EDGE + at, length)],
-            send_sem=piece_send.at[p], recv_sem=piece_recv.at[p],
-            device_id={"seq": here, "head": mate}, device_id_type=MESH,
-        )
-
-    def push(i, _):
-        piece(PIECES - 1 - i).start()
-        return 0
-
-    lax.fori_loop(0, PIECES, push, 0)
+    own_dt.start()
+    own_bc.start()
+    own_x.start()
+    own_w.start()
+    own_dt.wait()
 
     all_heads = dt_ref.shape[0]
     row8, head8 = iota((8, all_heads), 0), iota((8, all_heads), 1)
@@ -141,26 +114,59 @@
     per = width // HEADS
     head_row, head_col = iota((chunks * 8, width), 0) & 7, iota((chunks * 8, width), 1) // per
     to_chunk = (iota((chunks, chunks * 8), 1) // 8 == iota((chunks, chunks * 8), 0)).astype(F32)
-    totals = []
     for offset, where in ((0, exf), (HEADS, exr)):
         wide = jnp.where(head_row == head_col + offset, half, 0.0)
         summed = jnp.dot(to_chunk, wide, precision=HIGHEST, preferred_element_type=F32)
         where[...] = jnp.exp(summed)
-        totals.append(jnp.exp(2.0 * jnp.sum(summed, axis=0, keepdims=True)))
     gain = jnp.sum(
         jnp.where(iota((8, width), 0) == iota((8, width), 1) // per, gain8, 0.0), axis=0, keepdims=True
     )
     sel_row, sel_col = iota((16, width), 0) & 7, iota((16, width), 1) // per
     select_f = (sel_row == sel_col).astype(F32).astype(BF16)
     select_r = (sel_row == sel_col + HEADS).astype(F32).astype(BF16)
-    decay = jnp.where(iota((8, width), 0) == 0, totals[0], totals[1])
+    all_logs = sum(half[8 * k : 8 * k + 8, :] for k in range(chunks))
+    decay = jnp.broadcast_to(jnp.exp(2.0 * all_logs), (8, Q))
+    pl.semaphore_wait(barrier, seqs + 2)
+
+    def halo(i, src, dst, s, h):
+        return pltpu.make_async_remote_copy(
+            src_ref=src, dst_ref=dst, send_sem=halo_send.at[i], recv_sem=halo_recv.at[i],
+            device_id={"seq": s, "head": h}, device_id_type=MESH,
+        )
+
+    first, last = pl.ds(0, EDGE), pl.ds(rows - EDGE, EDGE)
+    low, high = pl.ds(0, EDGE), pl.ds(rows + EDGE, EDGE)
+    halos = [
+        halo(0, bc_hbm.at[last], pb.at[low], after, mine),
+        halo(1, bc_hbm.at[first], pb.at[high], before, mine),
+        halo(2, x_hbm.at[last], px.at[low], after, mine),
+        halo(3, x_hbm.at[first], pm.at[high], before, mate),
+    ]
+    for copy in halos:
+        copy.start()
+    length = rows // PIECES
+
+    def piece(p):
+        at = pl.multiple_of(p * length, length)
+        return pltpu.make_async_remote_copy(
+            src_ref=x_hbm.at[pl.ds(at, length)], dst_ref=pm.at[pl.ds(EDGE + at, length)],
+            send_sem=piece_send.at[p], recv_sem=piece_recv.at[p],
+            device_id={"seq": here, "head": mate}, device_id_type=MESH,
+        )
+
+    def push(i, _):
+        piece(PIECES - 1 - i).start()
+        return 0
+
+    lax.fori_loop(0, PIECES, push, 0)
+
     dmsg[...] = decay
     dall[here] = decay
 
     def tell(d):
         return pltpu.make_async_remote_copy(
-            src_ref=dmsg, dst_ref=dall.at[here], send_sem=d_send.at[d], recv_sem=d_recv.at[d],
-            device_id={"seq": lax.rem(here + d, seqs), "head": mine}, device_id_type=MESH,
+            src_ref=dmsg, dst_ref=dall.at[here], send_sem=d_send, recv_sem=d_recv,
+            device_id={"seq": (here + d) & (seqs - 1), "head": mine}, device_id_type=MESH,
         )
 
     def tell_start(d, _):
@@ -169,7 +175,8 @@
 
     lax.fori_loop(1, seqs, tell_start, 0)
 
-    weights_x = wx_ref[:, pl.ds(pl.multiple_of(mine * width, width), width)]
+    own_w.wait()
+    weights_x = wx_ref[...]
     weights_s = ws_ref[...]
 
     own_x.wait()
@@ -211,23 +218,27 @@
     stot[0] = lax.fori_loop(0, chunks, step_forward, jnp.zeros((Q, width), F32))
 
     def to_owner(way, d):
-        peer = lax.rem(here + d, seqs)
+        peer = (here + d) & (seqs - 1)
         return pltpu.make_async_remote_copy(
             src_ref=stot.at[way, pl.ds(pl.multiple_of(peer * share, share), share)],
-            dst_ref=ra.at[way, here], send_sem=a_send.at[way, d], recv_sem=a_recv.at[way, d],
+            dst_ref=ra.at[way, here], send_sem=a_send.at[way], recv_sem=a_recv.at[way],
             device_id={"seq": peer, "head": mine}, device_id_type=MESH,
         )
 
     def from_owner(way, d):
-        peer = lax.rem(here + d, seqs)
+        peer = (here + d) & (seqs - 1)
         return pltpu.make_async_remote_copy(
             src_ref=inc.at[way, peer],
             dst_ref=sin.at[way, pl.ds(pl.multiple_of(here * share, share), share)],
-            send_sem=b_send.at[way, d], recv_sem=b_recv.at[way, d],
+            send_sem=b_send.at[way], recv_sem=b_recv.at[way],
             device_id={"seq": peer, "head": mine}, device_id_type=MESH,
         )
 
     mine_rows = pl.ds(pl.multiple_of(here * share, share), share)
+
+    def others(buffer, way, sem):
+        span = buffer.at[way, pl.ds(0, seqs - 1)]
+        pltpu.make_async_copy(span, span, sem.at[way]).wait()
 
     def states_out(way):
         def go(d, _):
@@ -238,16 +249,15 @@
         ra[way, here] = stot[way, mine_rows, :]
 
     def states_back(way):
-        def arrive(d, _):
-            to_owner(way, d).wait_recv()
-            return 0
-
-        lax.fori_loop(1, seqs, arrive, 0)
+        others(ra, way, a_recv)
+        left = iota((1, Q), 1) < Q // 2
 
         def hop(i, entering):
             at = i if way == 0 else seqs - 1 - i
             inc[way, at] = entering
-            return dall[at, way : way + 1, :] * entering + ra[way, at]
+            d = [dall[at, HEADS * way + h : HEADS * way + h + 1, :] for h in range(HEADS)]
+            decay = jnp.concatenate([jnp.where(left, d[0], d[1]), jnp.where(left, d[2], d[3])], axis=1)
+            return decay * entering + ra[way, at]
 
         lax.fori_loop(0, seqs, hop, jnp.zeros((share, width), F32))
 
@@ -259,11 +269,7 @@
         sin[way, mine_rows, :] = inc[way, here]
 
     def states_in(way):
-        def arrive(d, _):
-            from_owner(way, d).wait_recv()
-            return 0
-
-        lax.fori_loop(1, seqs, arrive, 0)
+        others(inc, way, b_recv)
 
     def step_reverse(k):
         at = pl.multiple_of(k * Q, Q)
@@ -301,15 +307,14 @@
     def _():
         pm[pl.ds(rows + EDGE, EDGE), :] = jnp.zeros((EDGE, width), BF16)
 
-    pieces(0, 2)
-
-    def told(d, _):
-        tell(d).wait_recv()
-        return 0
-
-    lax.fori_loop(1, seqs, told, 0)
+    pieces(0, PIECES // 2)
+
+    everyone = dall.at[pl.ds(0, seqs - 1)]
+    pltpu.make_async_copy(everyone, everyone, d_recv).wait()
     states_back(0)
-    pieces(2, 4)
+    pieces(PIECES // 2, PIECES)
+    stot[1] = run[...]
+    states_out(1)
     states_in(0)
 
     def finish_forward(k, state):
@@ -322,10 +327,7 @@
         yf[pl.ds(at, Q), :] = scale * y + gain * xf[pl.ds(at, Q), :]
         return e * (entering + uf[k])
 
-    lax.fori_loop(0, chunks, finish_forward, sin[0])
-    pieces(4, PIECES)
-    stot[1] = run[...]
-    states_out(1)
+    lax.fori_loop(0, chunks // 2, lambda i, st: finish_forward(2 * i + 1, finish_forward(2 * i, st)), sin[0])
     states_back(1)
     states_in(1)
 
@@ -341,25 +343,18 @@
         out_ref[pl.ds(at, Q), :] = (yf[pl.ds(at, Q), :] + back.astype(F32)).astype(BF16)
         return e * (entering + ur[k])
 
-    lax.fori_loop(0, chunks, finish_reverse, sin[1])
+    lax.fori_loop(0, chunks // 2, lambda i, st: finish_reverse(2 * i + 1, finish_reverse(2 * i, st)), sin[1])
 
     for copy in halos:
         copy.wait_send()
 
-    def sent_piece(p, _):
+    for p in range(PIECES):
         piece(p).wait_send()
-        return 0
-
-    lax.fori_loop(0, PIECES, sent_piece, 0)
-
-    def sent(d, _):
-        tell(d).wait_send()
-        for way in (0, 1):
-            to_owner(way, d).wait_send()
-            from_owner(way, d).wait_send()
-        return 0
-
-    lax.fori_loop(1, seqs, sent, 0)
+
+    pltpu.make_async_copy(everyone, everyone, d_send).wait()
+    for way in (0, 1):
+        others(ra, way, a_send)
+        others(inc, way, b_send)
 
 
 def per_device(inputs, bc_inputs, dt_raw, conv_inner, conv_state, log_rate, dt_bias, skip_gain):
@@ -373,10 +368,10 @@
     return pl.pallas_call(
         functools.partial(kernel, seqs, ways),
         out_shape=jax.ShapeDtypeStruct((rows, width), BF16),
-        in_specs=[anywhere, anywhere] + [vmem] * 6,
+        in_specs=[anywhere] * 4 + [vmem] * 4,
         out_specs=vmem,
         scratch_shapes=[
-            padded, padded, padded,
+            pltpu.VMEM(dt_raw.shape, BF16), pltpu.VMEM((4, width), F32), padded, padded, padded,
             pltpu.VMEM((rows, 2 * Q), BF16), pltpu.VMEM((rows, 2 * Q), BF16), pltpu.VMEM((rows, Q), BF16),
             pltpu.VMEM((chunks, 2 * Q, width), BF16), pltpu.VMEM((chunks, 2 * Q, width), BF16),
             pltpu.VMEM((rows, width), F32), pltpu.VMEM((rows, width), F32),
@@ -387,12 +382,12 @@
             pltpu.VMEM((Q, width), F32), pltpu.VMEM((2, Q, width), F32),
             pltpu.VMEM((2, seqs, share, width), F32), pltpu.VMEM((2, seqs, share, width), F32),
             pltpu.VMEM((2, Q, width), F32),
-            pltpu.VMEM((8, width), F32), pltpu.VMEM((seqs, 8, width), F32),
-            dma((2,)), dma((4,)), dma((4,)), dma((PIECES,)), dma((PIECES,)),
-            dma((seqs,)), dma((seqs,)), dma((2, seqs)), dma((2, seqs)), dma((2, seqs)), dma((2, seqs)),
+            pltpu.VMEM((8, Q), F32), pltpu.VMEM((seqs, 8, Q), F32),
+            dma((4,)), dma((4,)), dma((4,)), dma((PIECES,)), dma((PIECES,)),
+            dma, dma, dma((2,)), dma((2,)), dma((2,)), dma((2,)),
         ],
         compiler_params=pltpu.CompilerParams(
-            collective_id=0, has_side_effects=True, vmem_limit_bytes=48 * 2**20
+            collective_id=0, has_side_effects=True, vmem_limit_bytes=60 * 2**20
         ),
     )(
         inputs, bc_inputs, dt_raw, conv_inner, conv_state,

time: 67.7 us -> 56.6 us (0.84)
  Pallas kernels: 61.5 us -> 54.2 us
  local copies, waits for them, and re-layouts: 5.9 us -> 2.26 us
    pallas_call x1, Pallas kernels: 61.5 us -> 54.2 us  [per_device(): pl.pallas_call(functools.partial(kernel, seqs, ways), out_shape=jax.Shape...]
    unnamed x17 -> x1, local copies, waits for them, and re-layouts: 5.9 us -> 2.26 us
where the time goes in v2:
time: 56.6 us; the launch traced here: 56.4 us
  Pallas kernels  54.2 us (96%)
  local copies, waits for them, and re-layouts  2.26 us (4%)
    pallas_call x1, Pallas kernels, per_device(): pl.pallas_call(functools.partial(kernel, seqs, ways), out_shape=jax.Shape...  54.2 us
    unnamed x1, local copies, waits for them, and re-layouts  2.26 us

profile of v2, /device:TPU:8, one launch (start us, length us, event | category | flops | bytes accessed | tf_op | source)
XLA Modules:
  0.0 56.4 jit_solution(17363079853442138046)
XLA Ops:
  0.0 54.2 %shard_map.82 = bf16[2048,256]{1,0:T(8,128)(2,1)} custom-call(bf16[2048,256]{1,0:T(8,128)(2,1)} %x_hbm.1, bf16[2048,256]{1,0:T(8,128)(2,1)} %bc_hbm.1, bf16[64,2048]{1,0:T(8,128)(2,1)} %dt_hbm.1, f32[4,4096]{1,0:T(4,128)} %wx_hbm.1, f32[4,256]{1,0:T(4,128)} %ws_ref.1, f32[1,64]{1,0:T(1,128)} %bitcast.3, f32[1,64]{1,0:T(1,128)} %bitcast.4, f32[1,64]{1,0:T(1,128)} %bitcast.5), custom_call_target="tpu_custom_call" | custom-call | tf_op jit(solution)/shard_map/pallas_call | solution.py:368
  54.2 2.3 %copy.10 = bf16[2048,256]{1,0:T(8,128)(2,1)} copy(bf16[2048,256]{1,0:T(8,128)(2,1)} %shard_map.82) | data formatting | bytes 2097152

commit v3 on v2

v3 whole, which is shorter than its diff:
```python
import functools

import jax
import jax.numpy as jnp
from jax import lax
from jax.experimental import pallas as pl
from jax.experimental.pallas import tpu as pltpu
from jax.sharding import PartitionSpec as P

Q = 128
EDGE = 16
HEADS = 4
PIECES = 4
HIGHEST = lax.Precision.HIGHEST
MESH = pl.DeviceIdType.MESH
F32 = jnp.float32
BF16 = jnp.bfloat16


def iota(shape, dim):
    return lax.broadcasted_iota(jnp.int32, shape, dim)


def silu(v):
    h = 0.5 * v
    return h * jnp.tanh(h) + h


def taps(window, weights, begins):
    total = weights[0:1, :] * window[begins[0] : begins[0] + Q]
    for i in range(1, 4):
        total = total + weights[i : i + 1, :] * window[begins[i] : begins[i] + Q]
    return total


def dot(a, b):
    return jnp.dot(a, b, preferred_element_type=F32)


def dot_nt(a, b):
    return lax.dot_general(a, b, (((1,), (1,)), ((), ())), preferred_element_type=F32)


def spread(rows, select):
    high = rows.astype(BF16).astype(F32)
    parts = jnp.concatenate([high, rows - high], axis=0)
    return dot(parts.T.astype(BF16), select)


def kernel(
    seqs, ways,
    x_hbm, bc_hbm, dt_hbm, wx_hbm, ws_ref, rate_ref, bias_ref, gain_ref,
    out_ref,
    dt_ref, wx_ref, wm_ref, px, pb, pm, gcf, gcr, btr, xsf, xsr, xf, xr, uf, ur, yf, ef, ff, exf, exr,
    away, back_in, tot_f, tot_r, got_f, got_r, inc_f, inc_r, in_f, in_r, dmsg, dall,
    local_sem, halo_send, halo_recv, piece_send, piece_recv,
    out_send, out_recv, d_send, d_recv, a_send, a_recv, b_send, b_recv,
):
    rows, width = x_hbm.shape
    chunks = rows // Q
    share = Q // seqs
    wing = width // 2
    here, mine = lax.axis_index("seq"), lax.axis_index("head")
    mate = (mine + ways // 2) & (ways - 1)
    after, before = (here + 1) & (seqs - 1), (here - 1) & (seqs - 1)

    own_x = pltpu.make_async_copy(x_hbm, px.at[pl.ds(EDGE, rows)], local_sem.at[0])
    own_bc = pltpu.make_async_copy(bc_hbm, pb.at[pl.ds(EDGE, rows)], local_sem.at[1])
    own_dt = pltpu.make_async_copy(dt_hbm, dt_ref, local_sem.at[2])
    columns = pl.ds(pl.multiple_of(mine * width, width), width)
    theirs = pl.ds(pl.multiple_of(mate * width + wing, wing), wing)
    mate_w = pltpu.make_async_copy(wx_hbm.at[:, theirs], wm_ref, local_sem.at[4])
    own_w = pltpu.make_async_copy(wx_hbm.at[:, columns], wx_ref, local_sem.at[3])

    barrier = pltpu.get_barrier_semaphore()

    def greet(d, _):
        peer = (here + d) & (seqs - 1)
        pl.semaphore_signal(barrier, inc=1, device_id={"seq": peer, "head": mine}, device_id_type=MESH)
        return 0

    lax.fori_loop(1, seqs, greet, 0)
    for s in (here, after, before):
        pl.semaphore_signal(barrier, inc=1, device_id={"seq": s, "head": mate}, device_id_type=MESH)
    own_dt.start()
    own_bc.start()
    own_x.start()
    own_w.start()
    mate_w.start()
    own_dt.wait()

    all_heads = dt_ref.shape[0]
    row8, head8 = iota((8, all_heads), 0), iota((8, all_heads), 1)
    owner8 = jnp.where(row8 < 6, mine, mate) * HEADS + (row8 & (HEADS - 1))
    source8 = jnp.where((row8 == 4) | (row8 == 5), mate, mine) * HEADS + (row8 & (HEADS - 1))
    raw8 = dot((head8 == source8).astype(F32).astype(BF16), dt_ref[...])
    chosen = head8 == owner8

    def pick(values):
        return jnp.sum(jnp.where(chosen, values, 0.0), axis=1, keepdims=True)

    rate8 = pick(-jnp.exp(rate_ref[...]))
    gain8 = pick(gain_ref[...])
    pre = raw8 + pick(bias_ref[...])
    dt8 = jnp.maximum(pre, 0.0) + jnp.log1p(jnp.exp(-jnp.abs(pre)))
    dt = jnp.concatenate([dt8[:, k * Q : (k + 1) * Q] for k in range(chunks)], axis=0)
    logs8 = dt8 * rate8
    logs = jnp.concatenate([logs8[:, k * Q : (k + 1) * Q] for k in range(chunks)], axis=0)
    r, c = iota((Q, Q), 0), iota((Q, Q), 1)
    upto = jnp.dot(logs, (r <= c).astype(F32), precision=HIGHEST, preferred_element_type=F32)
    onward = jnp.dot(logs, (r >= c).astype(F32), precision=HIGHEST, preferred_element_type=F32)
    is_forward = (iota((chunks * 8, Q), 0) & 7) < HEADS
    cum = jnp.where(is_forward, upto, onward)
    half = 0.5 * jnp.sum(logs, axis=1, keepdims=True)
    ef[...] = jnp.exp(cum - half)
    ff[...] = dt * jnp.exp(half - cum)
    per = width // HEADS
    head_row, head_col = iota((chunks * 8, width), 0) & 7, iota((chunks * 8, width), 1) // per
    to_chunk = (iota((chunks, chunks * 8), 1) // 8 == iota((chunks, chunks * 8), 0)).astype(F32)
    for offset, where in ((0, exf), (HEADS, exr)):
        wide = jnp.where(head_row == head_col + offset, half, 0.0)
        summed = jnp.dot(to_chunk, wide, precision=HIGHEST, preferred_element_type=F32)
        where[...] = jnp.exp(summed)
    gain_row, gain_col = iota((8, width), 0), iota((8, width), 1) // per
    gain_f = jnp.sum(jnp.where(gain_row == gain_col, gain8, 0.0), axis=0, keepdims=True)
    gain_r = jnp.sum(jnp.where(gain_row == gain_col + HEADS, gain8, 0.0), axis=0, keepdims=True)
    sel_row, sel_col = iota((16, width), 0) & 7, iota((16, width), 1) // per
    select_f = (sel_row == sel_col).astype(F32).astype(BF16)
    select_r = (sel_row == sel_col + HEADS).astype(F32).astype(BF16)
    all_logs = sum(half[8 * k : 8 * k + 8, :] for k in range(chunks))
    decay = jnp.broadcast_to(jnp.exp(2.0 * all_logs), (8, Q))
    pl.semaphore_wait(barrier, seqs + 2)

    def halo(i, src, dst, s, h):
        return pltpu.make_async_remote_copy(
            src_ref=src, dst_ref=dst, send_sem=halo_send.at[i], recv_sem=halo_recv.at[i],
            device_id={"seq": s, "head": h}, device_id_type=MESH,
        )

    first, last = pl.ds(0, EDGE), pl.ds(rows - EDGE, EDGE)
    low, high = pl.ds(0, EDGE), pl.ds(rows + EDGE, EDGE)
    halos = [
        halo(0, bc_hbm.at[last], pb.at[low], after, mine),
        halo(1, bc_hbm.at[first], pb.at[high], before, mine),
        halo(2, x_hbm.at[last], px.at[low], after, mine),
        halo(3, x_hbm.at[first], px.at[high], before, mine),
        halo(4, x_hbm.at[first, pl.ds(0, wing)], pm.at[high], before, mate),
    ]
    for copy in halos:
        copy.start()
    length = rows // PIECES

    def piece(p):
        at = pl.multiple_of(p * length, length)
        return pltpu.make_async_remote_copy(
            src_ref=x_hbm.at[pl.ds(at, length), pl.ds(0, wing)], dst_ref=pm.at[pl.ds(EDGE + at, length)],
            send_sem=piece_send.at[p], recv_sem=piece_recv.at[p],
            device_id={"seq": here, "head": mate}, device_id_type=MESH,
        )

    def push(i, _):
        piece(PIECES - 1 - i).start()
        return 0

    lax.fori_loop(0, PIECES, push, 0)

    dmsg[...] = decay
    dall[here] = decay

    def tell(d):
        return pltpu.make_async_remote_copy(
            src_ref=dmsg, dst_ref=dall.at[here], send_sem=d_send, recv_sem=d_recv,
            device_id={"seq": (here + d) & (seqs - 1), "head": mine}, device_id_type=MESH,
        )

    def tell_start(d, _):
        tell(d).start()
        return 0

    lax.fori_loop(1, seqs, tell_start, 0)

    own_w.wait()
    mate_w.wait()
    weights_x = wx_ref[...]
    weights_r = (weights_x[:, :wing], wm_ref[...])
    weights_s = ws_ref[...]

    own_x.wait()
    own_bc.wait()
    def by(n, body):
        def several(i, state):
            for j in range(n):
                state = body(n * i + j, state)
            return state

        return several

    def arrive_halos():
        for i in range(4):
            halos[i].wait_recv()

        @pl.when(here == 0)
        def _():
            px[pl.ds(0, EDGE), :] = jnp.zeros((EDGE, width), BF16)
            pb[pl.ds(0, EDGE), :] = jnp.zeros((EDGE, width), BF16)

        @pl.when(here == seqs - 1)
        def _():
            pb[pl.ds(rows + EDGE, EDGE), :] = jnp.zeros((EDGE, width), BF16)
            px[pl.ds(rows + EDGE, EDGE), :] = jnp.zeros((EDGE, width), BF16)

    def reverse_values(wing_index, source, column, k, map_t):
        at = pl.multiple_of(k * Q, Q)
        here_columns = slice(wing_index * wing, wing_index * wing + wing)
        window = source[pl.ds(EDGE + at, Q + EDGE), column : column + wing].astype(F32)
        value = silu(taps(window, weights_r[wing_index], [3, 2, 1, 0]))
        xr[wing_index, pl.ds(at, Q), :] = value
        steps = ff[pl.ds(pl.multiple_of(k * 8, 8), 8), :]
        scaled = (value * spread(steps, select_r[:, here_columns])).astype(BF16)
        xsr[wing_index, k] = scaled
        ur[wing_index, k] = dot(map_t, scaled)

    def reverse_total(wing_index):
        def step(i, state):
            k = chunks - 1 - i
            e = exr[pl.ds(k, 1), :][:, wing_index * wing : wing_index * wing + wing]
            return e * (e * state + ur[wing_index, k])

        tot_r[wing_index] = lax.fori_loop(0, chunks // 4, by(4, step), jnp.zeros((Q, wing), F32))

    def step_maps(k, _):
        at = pl.multiple_of(k * Q, Q)
        window = pb[pl.ds(EDGE + at, Q + EDGE), :Q].astype(F32)
        map_t = silu(taps(window, weights_s[:, :Q], [3, 2, 1, 0])).T.astype(BF16)
        btr[pl.ds(at, Q), :] = map_t
        reverse_values(1, px, wing, k, map_t)
        return 0

    def step_forward(k, state):
        at = pl.multiple_of(k * Q, Q)
        window = pb[pl.ds(at, Q + 2 * EDGE), :].astype(F32)
        cr = silu(taps(window[:, Q:], weights_s[:, Q:], [EDGE + 3, EDGE + 2, EDGE + 1, EDGE])).astype(BF16)
        gcr[pl.ds(at, Q), Q:] = cr
        gcr[pl.ds(at, Q), :Q] = jnp.where(r <= c, dot(cr, btr[pl.ds(at, Q), :]), 0.0).astype(BF16)
        fwd = silu(taps(window, weights_s, [EDGE - 3, EDGE - 2, EDGE - 1, EDGE]))
        bf, cf = fwd[:, :Q].astype(BF16), fwd[:, Q:].astype(BF16)
        gcf[pl.ds(at, Q), Q:] = cf
        gcf[pl.ds(at, Q), :Q] = jnp.where(r >= c, dot_nt(cf, bf), 0.0).astype(BF16)
        window = px[pl.ds(at, Q + EDGE), :].astype(F32)
        value = silu(taps(window, weights_x, [EDGE - 3, EDGE - 2, EDGE - 1, EDGE]))
        xf[pl.ds(at, Q), :] = value
        scaled = (value * spread(ff[pl.ds(pl.multiple_of(k * 8, 8), 8), :], select_f)).astype(BF16)
        xsf[k] = scaled
        uf[k] = dot(fwd[:, :Q].T.astype(BF16), scaled)
        return state

    def forward_total(k, state):
        e = exf[pl.ds(k, 1), :]
        return e * (e * state + uf[k])

    tot = (tot_f, tot_r.at[0], tot_r.at[1])
    got = (got_f, got_r.at[0], got_r.at[1])
    inc = (inc_f, inc_r.at[0], inc_r.at[1])
    into = (in_f, in_r.at[0], in_r.at[1])

    def to_owner(way, d):
        peer = (here + d) & (seqs - 1)
        return pltpu.make_async_remote_copy(
            src_ref=tot[way].at[pl.ds(pl.multiple_of(peer * share, share), share)],
            dst_ref=got[way].at[here], send_sem=a_send.at[way], recv_sem=a_recv.at[way],
            device_id={"seq": peer, "head": mine}, device_id_type=MESH,
        )

    def from_owner(way, d):
        peer = (here + d) & (seqs - 1)
        return pltpu.make_async_remote_copy(
            src_ref=inc[way].at[peer],
            dst_ref=into[way].at[pl.ds(pl.multiple_of(here * share, share), share)],
            send_sem=b_send.at[way], recv_sem=b_recv.at[way],
            device_id={"seq": peer, "head": mine}, device_id_type=MESH,
        )

    mine_rows = pl.ds(pl.multiple_of(here * share, share), share)

    def others(buffer, sem):
        span = buffer.at[pl.ds(0, seqs - 1)]
        pltpu.make_async_copy(span, span, sem).wait()

    def states_out(way):
        def go(d, _):
            to_owner(way, d).start()
            return 0

        lax.fori_loop(1, seqs, go, 0)
        got[way][here] = tot[way][mine_rows, :]

    left = iota((1, Q), 1) < Q // 2

    def states_back(way):
        others(got[way], a_recv.at[way])
        heads = ((0, 1, 2, 3), (4, 5), (6, 7))[way]

        def hop(i, entering):
            at = i if way == 0 else seqs - 1 - i
            inc[way][at] = entering
            d = [dall[at, h : h + 1, :] for h in heads]
            decay = jnp.concatenate([jnp.where(left, d[i], d[i + 1]) for i in range(0, len(d), 2)], axis=1)
            return decay * entering + got[way][at]

        lax.fori_loop(0, seqs, hop, jnp.zeros(got[way].shape[1:], F32))

        def go(d, _):
            from_owner(way, d).start()
            return 0

        lax.fori_loop(1, seqs, go, 0)
        into[way][mine_rows, :] = inc[way][here]

    def states_in(way):
        others(inc[way], b_recv.at[way])

    each = chunks // PIECES

    def pieces(start, stop):
        def one(i, _):
            p = PIECES - 1 - i
            piece(p).wait_recv()

            for j in range(each):
                k = p * each + each - 1 - j
                reverse_values(0, pm, 0, k, btr[pl.ds(pl.multiple_of(k * Q, Q), Q), :])
            return 0

        lax.fori_loop(start, stop, one, 0)

    def rebound(p):
        at = pl.multiple_of(p * length, length)
        return pltpu.make_async_remote_copy(
            src_ref=away.at[pl.ds(at, length)], dst_ref=back_in.at[pl.ds(at, length)],
            send_sem=out_send.at[p], recv_sem=out_recv.at[p],
            device_id={"seq": here, "head": mate}, device_id_type=MESH,
        )

    def finish_reverse(wing_index, k, state):
        at = pl.multiple_of(k * Q, Q)
        here_columns = slice(wing_index * wing, wing_index * wing + wing)
        e = exr[pl.ds(k, 1), :][:, here_columns]
        entering = e * state
        y = dot(gcr[pl.ds(at, Q), :], jnp.concatenate([xsr[wing_index, k], entering.astype(BF16)], axis=0))
        scale = spread(ef[pl.ds(pl.multiple_of(k * 8, 8), 8), :], select_r[:, here_columns])
        skip = gain_r[:, here_columns] * xr[wing_index, pl.ds(at, Q), :]
        return (scale * y + skip).astype(BF16), e * (entering + ur[wing_index, k])

    def finish_away(i, state):
        p = PIECES - 1 - i
        for j in range(each):
            k = p * each + each - 1 - j
            rounded, state = finish_reverse(1, k, state)
            away[pl.ds(pl.multiple_of(k * Q, Q), Q), :] = rounded
        rebound(p).start()
        return state

    def finish_forward(k, state):
        at = pl.multiple_of(k * Q, Q)
        e = exf[pl.ds(k, 1), :]
        entering = e * state
        y = dot(gcf[pl.ds(at, Q), :], jnp.concatenate([xsf[k], entering.astype(BF16)], axis=0))
        scale = spread(ef[pl.ds(pl.multiple_of(k * 8, 8), 8), :], select_f)
        yf[pl.ds(at, Q), :] = scale * y + gain_f * xf[pl.ds(at, Q), :]
        return e * (entering + uf[k])

    def finish_home(i, state):
        for j in range(4):
            k = chunks - 1 - 4 * i - j
            at = pl.multiple_of(k * Q, Q)
            rounded, state = finish_reverse(0, k, state)
            out_ref[pl.ds(at, Q), :wing] = (yf[pl.ds(at, Q), :wing] + rounded.astype(F32)).astype(BF16)
        return state

    def add_returned(i, _):
        p = PIECES - 1 - i
        rebound(p).wait_recv()
        at = pl.ds(pl.multiple_of(p * length, length), length)
        out_ref[at, wing:] = (yf[at, wing:] + back_in[at, :].astype(F32)).astype(BF16)
        return 0

    lax.fori_loop(0, chunks // 4 - 1, by(4, step_maps), 0)
    arrive_halos()
    lax.fori_loop(chunks // 4 - 1, chunks // 4, by(4, step_maps), 0)
    reverse_total(1)
    states_out(2)
    lax.fori_loop(0, chunks // 4, by(4, step_forward), 0)
    tot_f[...] = lax.fori_loop(0, chunks // 4, by(4, forward_total), jnp.zeros((Q, width), F32))
    states_out(0)
    everyone = dall.at[pl.ds(0, seqs - 1)]
    pltpu.make_async_copy(everyone, everyone, d_recv).wait()
    states_back(2)
    halos[4].wait_recv()

    @pl.when(here == seqs - 1)
    def _():
        pm[pl.ds(rows + EDGE, EDGE), :] = jnp.zeros((EDGE, wing), BF16)

    pieces(0, PIECES)
    reverse_total(0)
    states_out(1)
    states_back(0)
    states_in(2)
    lax.fori_loop(0, PIECES, finish_away, in_r[1])
    states_back(1)
    states_in(0)
    lax.fori_loop(0, chunks // 4, by(4, finish_forward), in_f[...])
    states_in(1)
    lax.fori_loop(0, chunks // 4, finish_home, in_r[0])
    lax.fori_loop(0, PIECES, add_returned, 0)

    for copy in halos:
        copy.wait_send()

    for p in range(PIECES):
        piece(p).wait_send()
        rebound(p).wait_send()

    pltpu.make_async_copy(everyone, everyone, d_send).wait()
    for way in range(3):
        others(got[way], a_send.at[way])
        others(inc[way], b_send.at[way])


def per_device(inputs, bc_inputs, dt_raw, conv_inner, conv_state, log_rate, dt_bias, skip_gain):
    seqs, ways = lax.axis_size("seq"), lax.axis_size("head")
    rows, width = inputs.shape
    chunks, share, wing = rows // Q, Q // seqs, width // 2
    anywhere = pl.BlockSpec(memory_space=pl.ANY)
    vmem = pl.BlockSpec(memory_space=pltpu.VMEM)
    padded = pltpu.VMEM((rows + 2 * EDGE, width), BF16)
    dma = pltpu.SemaphoreType.DMA
    return pl.pallas_call(
        functools.partial(kernel, seqs, ways),
        out_shape=jax.ShapeDtypeStruct((rows, width), BF16),
        in_specs=[anywhere] * 4 + [vmem] * 4,
        out_specs=vmem,
        scratch_shapes=[
            pltpu.VMEM(dt_raw.shape, BF16), pltpu.VMEM((4, width), F32), pltpu.VMEM((4, wing), F32),
            padded, padded, pltpu.VMEM((rows + 2 * EDGE, wing), BF16),
            pltpu.VMEM((rows, 2 * Q), BF16), pltpu.VMEM((rows, 2 * Q), BF16), pltpu.VMEM((rows, Q), BF16),
            pltpu.VMEM((chunks, Q, width), BF16), pltpu.VMEM((2, chunks, Q, wing), BF16),
            pltpu.VMEM((rows, width), F32), pltpu.VMEM((2, rows, wing), F32),
            pltpu.VMEM((chunks, Q, width), F32), pltpu.VMEM((2, chunks, Q, wing), F32),
            pltpu.VMEM((rows, width), F32),
            pltpu.VMEM((chunks * 8, Q), F32), pltpu.VMEM((chunks * 8, Q), F32),
            pltpu.VMEM((chunks, width), F32), pltpu.VMEM((chunks, width), F32),
            pltpu.VMEM((rows, wing), BF16), pltpu.VMEM((rows, wing), BF16),
            pltpu.VMEM((Q, width), F32), pltpu.VMEM((2, Q, wing), F32),
            pltpu.VMEM((seqs, share, width), F32), pltpu.VMEM((2, seqs, share, wing), F32),
            pltpu.VMEM((seqs, share, width), F32), pltpu.VMEM((2, seqs, share, wing), F32),
            pltpu.VMEM((Q, width), F32), pltpu.VMEM((2, Q, wing), F32),
            pltpu.VMEM((8, Q), F32), pltpu.VMEM((seqs, 8, Q), F32),
            dma((5,)), dma((5,)), dma((5,)), dma((PIECES,)), dma((PIECES,)), dma((PIECES,)), dma((PIECES,)),
            dma, dma, dma((3,)), dma((3,)), dma((3,)), dma((3,)),
        ],
        compiler_params=pltpu.CompilerParams(
            collective_id=0, has_side_effects=True, vmem_limit_bytes=60 * 2**20
        ),
    )(
        inputs, bc_inputs, dt_raw, conv_inner, conv_state,
        log_rate[None, :], dt_bias[None, :], skip_gain[None, :],
    )


def solution(mesh):
    return jax.shard_map(
        per_device,
        mesh=mesh,
        in_specs=(P("seq", "head"), P("seq", None), P(None, "seq"), P(), P(), P(), P(), P()),
        out_specs=P("seq", "head"),
        check_vma=False,
    )
```

time: 56.6 us -> 46.3 us (0.82)
  Pallas kernels: 54.2 us -> 43.4 us
    pallas_call x1, Pallas kernels: 54.2 us -> 43.4 us  [per_device(): pl.pallas_call(functools.partial(kernel, seqs, ways), out_shape=jax.Shape...]
where the time goes in v3:
time: 46.3 us; the launch traced here: 45.6 us
  Pallas kernels  43.4 us (94%)
  local copies, waits for them, and re-layouts  2.26 us (5%)
    pallas_call x1, Pallas kernels, per_device(): pl.pallas_call(functools.partial(kernel, seqs, ways), out_shape=jax.Shape...  43.4 us
    unnamed x1, local copies, waits for them, and re-layouts  2.26 us

profile of v3, /device:TPU:8, one launch (start us, length us, event | category | flops | bytes accessed | tf_op | source)
XLA Modules:
  0.0 45.6 jit_solution(9751996830538048900)
XLA Ops:
  0.0 43.4 %shard_map.82 = bf16[2048,256]{1,0:T(8,128)(2,1)} custom-call(bf16[2048,256]{1,0:T(8,128)(2,1)} %x_hbm.1, bf16[2048,256]{1,0:T(8,128)(2,1)} %bc_hbm.1, bf16[64,2048]{1,0:T(8,128)(2,1)} %dt_hbm.1, f32[4,4096]{1,0:T(4,128)} %wx_hbm.1, f32[4,256]{1,0:T(4,128)} %ws_ref.1, f32[1,64]{1,0:T(1,128)} %bitcast.3, f32[1,64]{1,0:T(1,128)} %bitcast.4, f32[1,64]{1,0:T(1,128)} %bitcast.5), custom_call_target="tpu_custom_call" | custom-call | tf_op jit(solution)/shard_map/pallas_call | solution.py:438
  43.4 2.3 %copy.10 = bf16[2048,256]{1,0:T(8,128)(2,1)} copy(bf16[2048,256]{1,0:T(8,128)(2,1)} %shard_map.82) | data formatting | bytes 2097152

commit v4 on v3

v4 whole, which is shorter than its diff:
```python
import functools

import jax
import jax.numpy as jnp
from jax import lax
from jax.experimental import pallas as pl
from jax.experimental.pallas import tpu as pltpu
from jax.sharding import PartitionSpec as P

Q = 128
EDGE = 16
HEADS = 4
PIECES = 8
TAIL = 2
HIGHEST = lax.Precision.HIGHEST
MESH = pl.DeviceIdType.MESH
F32 = jnp.float32
BF16 = jnp.bfloat16


def iota(shape, dim):
    return lax.broadcasted_iota(jnp.int32, shape, dim)


def silu(v):
    h = 0.5 * v
    return h * jnp.tanh(h) + h


def taps(window, weights, begins):
    total = weights[0:1, :] * window[begins[0] : begins[0] + Q]
    for i in range(1, 4):
        total = total + weights[i : i + 1, :] * window[begins[i] : begins[i] + Q]
    return total


def dot(a, b):
    return jnp.dot(a, b, preferred_element_type=F32)


def dot_nt(a, b):
    return lax.dot_general(a, b, (((1,), (1,)), ((), ())), preferred_element_type=F32)


def spread(rows, select):
    high = rows.astype(BF16).astype(F32)
    parts = jnp.concatenate([high, rows - high], axis=0)
    return dot(parts.T.astype(BF16), select)


def kernel(
    seqs, ways,
    x_hbm, bc_hbm, dt_hbm, wx_hbm, ws_ref, rate_ref, bias_ref, gain_ref,
    out_ref,
    dt_ref, wx_ref, wm_ref, px, pb, pm, gcf, gcr, btr, xsf, xsr, xf, xr, uf, ur, yf, ef, ff, er, fr, exf, exm, exr,
    back, tot_f, tot_r, got_f, got_r, inc_f, inc_r, in_f, in_r, dmsg, dall,
    local_sem, halo_send, halo_recv, piece_send, piece_recv,
    d_send, d_recv, a_send, a_recv, b_send, b_recv,
):
    rows, width = x_hbm.shape
    chunks = rows // Q
    share = Q // seqs
    wing = width // 2
    here, mine = lax.axis_index("seq"), lax.axis_index("head")
    mate = (mine + ways // 2) & (ways - 1)
    after, before = (here + 1) & (seqs - 1), (here - 1) & (seqs - 1)

    own_x = pltpu.make_async_copy(x_hbm, px.at[pl.ds(EDGE, rows)], local_sem.at[0])
    own_bc = pltpu.make_async_copy(bc_hbm, pb.at[pl.ds(EDGE, rows)], local_sem.at[1])
    own_dt = pltpu.make_async_copy(dt_hbm, dt_ref, local_sem.at[2])
    columns = pl.ds(pl.multiple_of(mine * width, width), width)
    theirs = pl.ds(pl.multiple_of(mate * width, width), width)
    mate_w = pltpu.make_async_copy(wx_hbm.at[:, theirs], wm_ref, local_sem.at[4])
    own_w = pltpu.make_async_copy(wx_hbm.at[:, columns], wx_ref, local_sem.at[3])

    barrier = pltpu.get_barrier_semaphore()

    def greet(d, _):
        peer = (here + d) & (seqs - 1)
        pl.semaphore_signal(barrier, inc=1, device_id={"seq": peer, "head": mine}, device_id_type=MESH)
        return 0

    def greet_mate(d, _):
        peer = (here + d) & (seqs - 1)
        pl.semaphore_signal(barrier, inc=1, device_id={"seq": peer, "head": mate}, device_id_type=MESH)
        return 0

    lax.fori_loop(1, seqs, greet, 0)
    lax.fori_loop(0, seqs, greet_mate, 0)
    own_dt.start()
    own_bc.start()
    own_x.start()
    own_w.start()
    mate_w.start()
    pl.semaphore_wait(barrier, 2 * seqs - 1)

    def halo(i, src, dst, s, h):
        return pltpu.make_async_remote_copy(
            src_ref=src, dst_ref=dst, send_sem=halo_send.at[i], recv_sem=halo_recv.at[i],
            device_id={"seq": s, "head": h}, device_id_type=MESH,
        )

    first, last = pl.ds(0, EDGE), pl.ds(rows - EDGE, EDGE)
    low, high = pl.ds(0, EDGE), pl.ds(rows + EDGE, EDGE)
    halos = [
        halo(0, bc_hbm.at[last], pb.at[low], after, mine),
        halo(1, bc_hbm.at[first], pb.at[high], before, mine),
        halo(2, x_hbm.at[last], px.at[low], after, mine),
        halo(3, x_hbm.at[first], px.at[high], before, mine),
        halo(4, x_hbm.at[first], pm.at[high], before, mate),
    ]
    for copy in halos:
        copy.start()
    length = rows // PIECES

    def piece(p):
        at = pl.multiple_of(p * length, length)
        return pltpu.make_async_remote_copy(
            src_ref=x_hbm.at[pl.ds(at, length)], dst_ref=pm.at[pl.ds(EDGE + at, length)],
            send_sem=piece_send.at[p], recv_sem=piece_recv.at[p],
            device_id={"seq": here, "head": mate}, device_id_type=MESH,
        )

    def push(i, _):
        piece(PIECES - 1 - i).start()
        return 0

    lax.fori_loop(0, 6, push, 0)

    own_dt.wait()

    all_heads = dt_ref.shape[0]
    row8, head8 = iota((8, all_heads), 0), iota((8, all_heads), 1)
    r, c = iota((Q, Q), 0), iota((Q, Q), 1)
    per = width // HEADS
    head_row, head_col = iota((chunks * 8, width), 0) & 7, iota((chunks * 8, width), 1) // per
    to_chunk = (iota((chunks, chunks * 8), 1) // 8 == iota((chunks, chunks * 8), 0)).astype(F32)

    def pick(owner8, values):
        return jnp.sum(jnp.where(head8 == owner8, values, 0.0), axis=1, keepdims=True)

    def stack(values):
        return jnp.concatenate([values[:, k * Q : (k + 1) * Q] for k in range(chunks)], axis=0)

    def steps_of(owner8, source8, forwards, e_ref, f_ref):
        raw8 = dot((head8 == source8).astype(F32).astype(BF16), dt_ref[...])
        rate8 = pick(owner8, -jnp.exp(rate_ref[...]))
        pre = raw8 + pick(owner8, bias_ref[...])
        dt8 = jnp.maximum(pre, 0.0) + jnp.log1p(jnp.exp(-jnp.abs(pre)))
        logs = stack(dt8 * rate8)
        cum = jnp.dot(logs, (r >= c).astype(F32), precision=HIGHEST, preferred_element_type=F32)
        if forwards:
            upto = jnp.dot(logs, (r <= c).astype(F32), precision=HIGHEST, preferred_element_type=F32)
            cum = jnp.where((iota((chunks * 8, Q), 0) & 7) < forwards, upto, cum)
        half = 0.5 * jnp.sum(logs, axis=1, keepdims=True)
        e_ref[...] = jnp.exp(cum - half)
        f_ref[...] = stack(dt8) * jnp.exp(half - cum)
        return half

    def chunk_decay(half, offset):
        wide = jnp.where(head_row == head_col + offset, half, 0.0)
        return jnp.exp(jnp.dot(to_chunk, wide, precision=HIGHEST, preferred_element_type=F32))

    local = row8 & (HEADS - 1)
    own8 = mine * HEADS + local
    half = steps_of(jnp.where(row8 < HEADS, mine, mate) * HEADS + local, own8, HEADS, ef, ff)
    exf[...] = chunk_decay(half, 0)
    exm[...] = chunk_decay(half, HEADS)
    gain = jnp.sum(
        jnp.where(iota((8, width), 0) == iota((8, width), 1) // per, pick(own8, gain_ref[...]), 0.0),
        axis=0, keepdims=True,
    )
    sel_row, sel_col = iota((16, width), 0) & 7, iota((16, width), 1) // per
    select_f = (sel_row == sel_col).astype(F32).astype(BF16)
    select_r = (sel_row == sel_col + HEADS).astype(F32).astype(BF16)
    all_logs = sum(half[8 * k : 8 * k + 8, :] for k in range(chunks))
    decay = jnp.broadcast_to(jnp.exp(2.0 * all_logs), (8, Q))
    dmsg[...] = decay
    dall[here] = decay

    def tell(d):
        return pltpu.make_async_remote_copy(
            src_ref=dmsg, dst_ref=dall.at[here], send_sem=d_send, recv_sem=d_recv,
            device_id={"seq": (here + d) & (seqs - 1), "head": mine}, device_id_type=MESH,
        )

    def tell_start(d, _):
        tell(d).start()
        return 0

    lax.fori_loop(1, seqs, tell_start, 0)

    own_w.wait()
    mate_w.wait()
    weights_x = wx_ref[...]
    weights_m = wm_ref[...]
    weights_s = ws_ref[...]

    own_x.wait()
    own_bc.wait()
    def by(n, body):
        def several(i, state):
            for j in range(n):
                state = body(n * i + j, state)
            return state

        return several

    def arrive_halos():
        for i in range(4):
            halos[i].wait_recv()

        @pl.when(here == 0)
        def _():
            px[pl.ds(0, EDGE), :] = jnp.zeros((EDGE, width), BF16)
            pb[pl.ds(0, EDGE), :] = jnp.zeros((EDGE, width), BF16)

        @pl.when(here == seqs - 1)
        def _():
            pb[pl.ds(rows + EDGE, EDGE), :] = jnp.zeros((EDGE, width), BF16)
            px[pl.ds(rows + EDGE, EDGE), :] = jnp.zeros((EDGE, width), BF16)

    def reverse_total():
        def step(i, state):
            k = chunks - 1 - i
            e = exm[pl.ds(k, 1), :]
            return e * (e * state + ur[k])

        tot_r[...] = lax.fori_loop(0, chunks // 4, by(4, step), jnp.zeros((Q, width), F32))

    def step_mate(k, _):
        at = pl.multiple_of(k * Q, Q)
        window = pb[pl.ds(EDGE + at, Q + EDGE), :Q].astype(F32)
        map_t = silu(taps(window, weights_s[:, :Q], [3, 2, 1, 0])).T.astype(BF16)
        btr[pl.ds(at, Q), :] = map_t
        window = px[pl.ds(EDGE + at, Q + EDGE), :].astype(F32)
        value = silu(taps(window, weights_m, [3, 2, 1, 0]))
        scaled = value * spread(ff[pl.ds(pl.multiple_of(k * 8, 8), 8), :], select_r)
        ur[k] = dot(map_t, scaled.astype(BF16))
        return 0

    def step_maps(k, _):
        at = pl.multiple_of(k * Q, Q)
        window = pb[pl.ds(EDGE + at, Q + EDGE), Q:].astype(F32)
        cr = silu(taps(window, weights_s[:, Q:], [3, 2, 1, 0])).astype(BF16)
        gcr[pl.ds(at, Q), Q:] = cr
        gcr[pl.ds(at, Q), :Q] = jnp.where(r <= c, dot(cr, btr[pl.ds(at, Q), :]), 0.0).astype(BF16)
        return 0

    def step_reverse(k):
        at = pl.multiple_of(k * Q, Q)
        window = pm[pl.ds(EDGE + at, Q + EDGE), :].astype(F32)
        value = silu(taps(window, weights_x, [3, 2, 1, 0]))
        xr[pl.ds(at, Q), :] = value
        scaled = (value * spread(fr[pl.ds(pl.multiple_of(k * 8, 8), 8), :], select_f)).astype(BF16)
        xsr[k] = scaled
        ur[k] = dot(btr[pl.ds(at, Q), :], scaled)

    def step_forward(k, state):
        at = pl.multiple_of(k * Q, Q)
        window = pb[pl.ds(at, Q + EDGE), :].astype(F32)
        fwd = silu(taps(window, weights_s, [EDGE - 3, EDGE - 2, EDGE - 1, EDGE]))
        bf, cf = fwd[:, :Q].astype(BF16), fwd[:, Q:].astype(BF16)
        gcf[pl.ds(at, Q), Q:] = cf
        gcf[pl.ds(at, Q), :Q] = jnp.where(r >= c, dot_nt(cf, bf), 0.0).astype(BF16)
        window = px[pl.ds(at, Q + EDGE), :].astype(F32)
        value = silu(taps(window, weights_x, [EDGE - 3, EDGE - 2, EDGE - 1, EDGE]))
        xf[pl.ds(at, Q), :] = value
        scaled = (value * spread(ff[pl.ds(pl.multiple_of(k * 8, 8), 8), :], select_f)).astype(BF16)
        xsf[k] = scaled
        uf[k] = dot(fwd[:, :Q].T.astype(BF16), scaled)
        return state

    def forward_total(k, state):
        e = exf[pl.ds(k, 1), :]
        return e * (e * state + uf[k])

    tot, got, inc = (tot_f, tot_r), (got_f, got_r), (inc_f, inc_r)

    def to_owner(way, d):
        peer = (here + d) & (seqs - 1)
        return pltpu.make_async_remote_copy(
            src_ref=tot[way].at[pl.ds(pl.multiple_of(peer * share, share), share)],
            dst_ref=got[way].at[here], send_sem=a_send.at[way], recv_sem=a_recv.at[way],
            device_id={"seq": peer, "head": mine}, device_id_type=MESH,
        )

    def from_owner(way, d):
        peer = (here + d) & (seqs - 1)
        landing = in_f.at[pl.ds(pl.multiple_of(here * share, share), share)] if way == 0 else in_r.at[here]
        return pltpu.make_async_remote_copy(
            src_ref=inc[way].at[peer], dst_ref=landing,
            send_sem=b_send.at[way], recv_sem=b_recv.at[way],
            device_id={"seq": peer, "head": mine if way == 0 else mate}, device_id_type=MESH,
        )

    mine_rows = pl.ds(pl.multiple_of(here * share, share), share)

    def others(buffer, sem, count=seqs - 1):
        span = buffer.at[pl.ds(0, count)]
        pltpu.make_async_copy(span, span, sem).wait()

    def states_out(way):
        def go(d, _):
            to_owner(way, d).start()
            return 0

        lax.fori_loop(1, seqs, go, 0)
        got[way][here] = tot[way][mine_rows, :]

    left = iota((1, Q), 1) < Q // 2

    def states_back(way):
        others(got[way], a_recv.at[way])

        def hop(i, entering):
            at = i if way == 0 else seqs - 1 - i
            if way == 0:
                inc_f[at] = entering
            else:
                inc_r[at] = jnp.concatenate([entering[:, :wing], entering[:, wing:]], axis=0).astype(BF16)
            d = [dall[at, HEADS * way + h : HEADS * way + h + 1, :] for h in range(HEADS)]
            decay = jnp.concatenate([jnp.where(left, d[0], d[1]), jnp.where(left, d[2], d[3])], axis=1)
            return decay * entering + got[way][at]

        lax.fori_loop(0, seqs, hop, jnp.zeros(got[way].shape[1:], F32))

        def go(d, _):
            from_owner(way, d).start()
            return 0

        lax.fori_loop(1 - way, seqs, go, 0)
        if way == 0:
            in_f[mine_rows, :] = inc_f[here]

    def entered():
        others(in_r, b_recv.at[1], seqs)
        blocks = [in_r[j].astype(F32) for j in range(seqs)]
        return jnp.concatenate([jnp.concatenate([b[:share], b[share:]], axis=1) for b in blocks], axis=0)

    each = chunks // PIECES

    def pieces(start, stop):
        def one(i, _):
            p = PIECES - 1 - i
            piece(p).wait_recv()

            for j in range(each):
                k = p * each + each - 1 - j
                step_reverse(k)
            return 0

        lax.fori_loop(start, stop, one, 0)

    def finish_forward(k, state, early):
        at = pl.multiple_of(k * Q, Q)
        e = exf[pl.ds(k, 1), :]
        entering = e * state
        y = dot(gcf[pl.ds(at, Q), :], jnp.concatenate([xsf[k], entering.astype(BF16)], axis=0))
        scale = spread(ef[pl.ds(pl.multiple_of(k * 8, 8), 8), :], select_f)
        y = scale * y + gain * xf[pl.ds(at, Q), :]
        if early:
            out_ref[pl.ds(at, Q), :] = (y + back[pl.ds(at, Q), :].astype(F32)).astype(BF16)
        else:
            yf[pl.ds(at, Q), :] = y
        return e * (entering + uf[k])

    def finish_reverse(k, state):
        at = pl.multiple_of(k * Q, Q)
        e = exr[pl.ds(k, 1), :]
        entering = e * state
        y = dot(gcr[pl.ds(at, Q), :], jnp.concatenate([xsr[k], entering.astype(BF16)], axis=0))
        scale = spread(er[pl.ds(pl.multiple_of(k * 8, 8), 8), :], select_f)
        return (scale * y + gain * xr[pl.ds(at, Q), :]).astype(BF16), e * (entering + ur[k])

    def finish_early(i, state):
        k = chunks - 1 - i
        back[pl.ds(pl.multiple_of(k * Q, Q), Q), :], state = finish_reverse(k, state)
        return state

    late = TAIL * each

    lax.fori_loop(0, chunks // 4 - 1, by(4, step_mate), 0)
    arrive_halos()
    lax.fori_loop(chunks // 4 - 1, chunks // 4, by(4, step_mate), 0)
    reverse_total()
    states_out(1)
    lax.fori_loop(0, chunks // 4, by(4, step_forward), 0)
    tot_f[...] = lax.fori_loop(0, chunks // 4, by(4, forward_total), jnp.zeros((Q, width), F32))
    states_out(0)
    lax.fori_loop(0, chunks // 4, by(4, step_maps), 0)
    half = steps_of(own8, mate * HEADS + local, 0, er, fr)
    exr[...] = chunk_decay(half, 0)
    everyone = dall.at[pl.ds(0, seqs - 1)]
    pltpu.make_async_copy(everyone, everyone, d_recv).wait()
    states_back(1)
    lax.fori_loop(6, PIECES, push, 0)
    halos[4].wait_recv()

    @pl.when(here == seqs - 1)
    def _():
        pm[pl.ds(rows + EDGE, EDGE), :] = jnp.zeros((EDGE, width), BF16)

    pieces(0, PIECES // 2)
    states_back(0)
    pieces(PIECES // 2, PIECES - TAIL)
    state = lax.fori_loop(0, (chunks - late) // 4, by(4, finish_early), entered())
    others(inc_f, b_recv.at[0])
    forward = lax.fori_loop(0, late // 4, by(4, lambda k, st: finish_forward(k, st, False)), in_f[...])
    lax.fori_loop(late // 4, chunks // 4, by(4, lambda k, st: finish_forward(k, st, True)), forward)

    def finish_late(i, state):
        p = TAIL - 1 - i
        piece(p).wait_recv()
        ks = [p * each + each - 1 - j for j in range(each)]
        for k in ks:
            step_reverse(k)
        for k in ks:
            at = pl.multiple_of(k * Q, Q)
            rounded, state = finish_reverse(k, state)
            out_ref[pl.ds(at, Q), :] = (yf[pl.ds(at, Q), :] + rounded.astype(F32)).astype(BF16)
        return state

    lax.fori_loop(0, TAIL, finish_late, state)

    for copy in halos:
        copy.wait_send()

    for p in range(PIECES):
        piece(p).wait_send()

    pltpu.make_async_copy(everyone, everyone, d_send).wait()
    for way in (0, 1):
        others(got[way], a_send.at[way])
        others(inc[way], b_send.at[way], seqs - 1 + way)


def per_device(inputs, bc_inputs, dt_raw, conv_inner, conv_state, log_rate, dt_bias, skip_gain):
    seqs, ways = lax.axis_size("seq"), lax.axis_size("head")
    rows, width = inputs.shape
    chunks, share, wing = rows // Q, Q // seqs, width // 2
    anywhere = pl.BlockSpec(memory_space=pl.ANY)
    vmem = pl.BlockSpec(memory_space=pltpu.VMEM)
    padded = pltpu.VMEM((rows + 2 * EDGE, width), BF16)
    steps, decays = pltpu.VMEM((chunks * 8, Q), F32), pltpu.VMEM((chunks, width), F32)
    dma = pltpu.SemaphoreType.DMA
    return pl.pallas_call(
        functools.partial(kernel, seqs, ways),
        out_shape=jax.ShapeDtypeStruct((rows, width), BF16),
        in_specs=[anywhere] * 4 + [vmem] * 4,
        out_specs=vmem,
        scratch_shapes=[
            pltpu.VMEM(dt_raw.shape, BF16), pltpu.VMEM((4, width), F32), pltpu.VMEM((4, width), F32),
            padded, padded, padded,
            pltpu.VMEM((rows, 2 * Q), BF16), pltpu.VMEM((rows, 2 * Q), BF16), pltpu.VMEM((rows, Q), BF16),
            pltpu.VMEM((chunks, Q, width), BF16), pltpu.VMEM((chunks, Q, width), BF16),
            pltpu.VMEM((rows, width), F32), pltpu.VMEM((rows, width), F32),
            pltpu.VMEM((chunks, Q, width), F32), pltpu.VMEM((chunks, Q, width), F32),
            pltpu.VMEM((rows, width), F32),
            steps, steps, steps, steps, decays, decays, decays,
            pltpu.VMEM((rows, width), BF16), pltpu.VMEM((Q, width), F32), pltpu.VMEM((Q, width), F32),
            pltpu.VMEM((seqs, share, width), F32), pltpu.VMEM((seqs, share, width), F32),
            pltpu.VMEM((seqs, share, width), F32), pltpu.VMEM((seqs, 2 * share, wing), BF16),
            pltpu.VMEM((Q, width), F32), pltpu.VMEM((seqs, 2 * share, wing), BF16),
            pltpu.VMEM((8, Q), F32), pltpu.VMEM((seqs, 8, Q), F32),
            dma((5,)), dma((5,)), dma((5,)), dma((PIECES,)), dma((PIECES,)),
            dma, dma, dma((2,)), dma((2,)), dma((2,)), dma((2,)),
        ],
        compiler_params=pltpu.CompilerParams(
            collective_id=0, has_side_effects=True, vmem_limit_bytes=60 * 2**20
        ),
    )(
        inputs, bc_inputs, dt_raw, conv_inner, conv_state,
        log_rate[None, :], dt_bias[None, :], skip_gain[None, :],
    )


def solution(mesh):
    return jax.shard_map(
        per_device,
        mesh=mesh,
        in_specs=(P("seq", "head"), P("seq", None), P(None, "seq"), P(), P(), P(), P(), P()),
        out_specs=P("seq", "head"),
        check_vma=False,
    )
```

time: 46.3 us -> 43.5 us (0.940)
  Pallas kernels: 43.4 us -> 41 us
    pallas_call x1, Pallas kernels: 43.4 us -> 41 us  [per_device(): pl.pallas_call(functools.partial(kernel, seqs, ways), out_shape=jax.Shape...]
where the time goes in v4:
time: 43.5 us; the launch traced here: 43.2 us
  Pallas kernels  41 us (94%)
  local copies, waits for them, and re-layouts  2.26 us (5%)
    pallas_call x1, Pallas kernels, per_device(): pl.pallas_call(functools.partial(kernel, seqs, ways), out_shape=jax.Shape...  41 us
    unnamed x1, local copies, waits for them, and re-layouts  2.26 us

profile of v4, /device:TPU:8, one launch (start us, length us, event | category | flops | bytes accessed | tf_op | source)
XLA Modules:
  0.0 43.2 jit_solution(12828369523994968420)
XLA Ops:
  0.0 41.0 %shard_map.82 = bf16[2048,256]{1,0:T(8,128)(2,1)} custom-call(bf16[2048,256]{1,0:T(8,128)(2,1)} %x_hbm.1, bf16[2048,256]{1,0:T(8,128)(2,1)} %bc_hbm.1, bf16[64,2048]{1,0:T(8,128)(2,1)} %dt_hbm.1, f32[4,4096]{1,0:T(4,128)} %wx_hbm.1, f32[4,256]{1,0:T(4,128)} %ws_ref.1, f32[1,64]{1,0:T(1,128)} %bitcast.3, f32[1,64]{1,0:T(1,128)} %bitcast.4, f32[1,64]{1,0:T(1,128)} %bitcast.5), custom_call_target="tpu_custom_call" | custom-call | tf_op jit(solution)/shard_map/pallas_call | solution.py:447
  41.0 2.3 %copy.10 = bf16[2048,256]{1,0:T(8,128)(2,1)} copy(bf16[2048,256]{1,0:T(8,128)(2,1)} %shard_map.82) | data formatting | bytes 2097152

commit v5 on v4

--- a/solution.py
+++ b/solution.py
@@ -50,9 +50,9 @@
 
 def kernel(
     seqs, ways,
-    x_hbm, bc_hbm, dt_hbm, wx_hbm, ws_ref, rate_ref, bias_ref, gain_ref,
+    x_hbm, bc_hbm, dt_hbm, wx_hbm, ws_hbm, rate_hbm, bias_hbm, gain_hbm,
     out_ref,
-    dt_ref, wx_ref, wm_ref, px, pb, pm, gcf, gcr, btr, xsf, xsr, xf, xr, uf, ur, yf, ef, ff, er, fr, exf, exm, exr,
+    ws_ref, rate_ref, bias_ref, gain_ref, dt_ref, wx_ref, wm_ref, px, pb, pm, gcf, gcr, btr, btf, xsf, xsr, xf, xr, uf, ur, yf, ef, ff, er, fr, exf, exm, exr,
     back, tot_f, tot_r, got_f, got_r, inc_f, inc_r, in_f, in_r, dmsg, dall,
     local_sem, halo_send, halo_recv, piece_send, piece_recv,
     d_send, d_recv, a_send, a_recv, b_send, b_recv,
@@ -87,7 +87,15 @@
 
     lax.fori_loop(1, seqs, greet, 0)
     lax.fori_loop(0, seqs, greet_mate, 0)
+    small = [
+        pltpu.make_async_copy(source, target, local_sem.at[5 + i])
+        for i, (source, target) in enumerate(
+            ((rate_hbm, rate_ref), (bias_hbm, bias_ref), (gain_hbm, gain_ref), (ws_hbm, ws_ref))
+        )
+    ]
     own_dt.start()
+    for copy in small:
+        copy.start()
     own_bc.start()
     own_x.start()
     own_w.start()
@@ -128,6 +136,8 @@
     lax.fori_loop(0, 6, push, 0)
 
     own_dt.wait()
+    for copy in small:
+        copy.wait()
 
     all_heads = dt_ref.shape[0]
     row8, head8 = iota((8, all_heads), 0), iota((8, all_heads), 1)
@@ -241,8 +251,11 @@
 
     def step_maps(k, _):
         at = pl.multiple_of(k * Q, Q)
-        window = pb[pl.ds(EDGE + at, Q + EDGE), Q:].astype(F32)
-        cr = silu(taps(window, weights_s[:, Q:], [3, 2, 1, 0])).astype(BF16)
+        window = pb[pl.ds(at, Q + 2 * EDGE), Q:].astype(F32)
+        cf = silu(taps(window, weights_s[:, Q:], [EDGE - 3, EDGE - 2, EDGE - 1, EDGE])).astype(BF16)
+        gcf[pl.ds(at, Q), Q:] = cf
+        gcf[pl.ds(at, Q), :Q] = jnp.where(r >= c, dot(cf, btf[pl.ds(at, Q), :]), 0.0).astype(BF16)
+        cr = silu(taps(window, weights_s[:, Q:], [EDGE + 3, EDGE + 2, EDGE + 1, EDGE])).astype(BF16)
         gcr[pl.ds(at, Q), Q:] = cr
         gcr[pl.ds(at, Q), :Q] = jnp.where(r <= c, dot(cr, btr[pl.ds(at, Q), :]), 0.0).astype(BF16)
         return 0
@@ -258,17 +271,15 @@
 
     def step_forward(k, state):
         at = pl.multiple_of(k * Q, Q)
-        window = pb[pl.ds(at, Q + EDGE), :].astype(F32)
-        fwd = silu(taps(window, weights_s, [EDGE - 3, EDGE - 2, EDGE - 1, EDGE]))
-        bf, cf = fwd[:, :Q].astype(BF16), fwd[:, Q:].astype(BF16)
-        gcf[pl.ds(at, Q), Q:] = cf
-        gcf[pl.ds(at, Q), :Q] = jnp.where(r >= c, dot_nt(cf, bf), 0.0).astype(BF16)
+        window = pb[pl.ds(at, Q + EDGE), :Q].astype(F32)
+        map_t = silu(taps(window, weights_s[:, :Q], [EDGE - 3, EDGE - 2, EDGE - 1, EDGE])).T.astype(BF16)
+        btf[pl.ds(at, Q), :] = map_t
         window = px[pl.ds(at, Q + EDGE), :].astype(F32)
         value = silu(taps(window, weights_x, [EDGE - 3, EDGE - 2, EDGE - 1, EDGE]))
         xf[pl.ds(at, Q), :] = value
         scaled = (value * spread(ff[pl.ds(pl.multiple_of(k * 8, 8), 8), :], select_f)).astype(BF16)
         xsf[k] = scaled
-        uf[k] = dot(fwd[:, :Q].T.astype(BF16), scaled)
+        uf[k] = dot(map_t, scaled)
         return state
 
     def forward_total(k, state):
@@ -447,12 +458,15 @@
     return pl.pallas_call(
         functools.partial(kernel, seqs, ways),
         out_shape=jax.ShapeDtypeStruct((rows, width), BF16),
-        in_specs=[anywhere] * 4 + [vmem] * 4,
+        in_specs=[anywhere] * 8,
         out_specs=vmem,
         scratch_shapes=[
+            pltpu.VMEM(conv_state.shape, F32), pltpu.VMEM((1, log_rate.shape[0]), F32),
+            pltpu.VMEM((1, log_rate.shape[0]), F32), pltpu.VMEM((1, log_rate.shape[0]), F32),
             pltpu.VMEM(dt_raw.shape, BF16), pltpu.VMEM((4, width), F32), pltpu.VMEM((4, width), F32),
             padded, padded, padded,
-            pltpu.VMEM((rows, 2 * Q), BF16), pltpu.VMEM((rows, 2 * Q), BF16), pltpu.VMEM((rows, Q), BF16),
+            pltpu.VMEM((rows, 2 * Q), BF16), pltpu.VMEM((rows, 2 * Q), BF16),
+            pltpu.VMEM((rows, Q), BF16), pltpu.VMEM((rows, Q), BF16),
             pltpu.VMEM((chunks, Q, width), BF16), pltpu.VMEM((chunks, Q, width), BF16),
             pltpu.VMEM((rows, width), F32), pltpu.VMEM((rows, width), F32),
             pltpu.VMEM((chunks, Q, width), F32), pltpu.VMEM((chunks, Q, width), F32),
@@ -463,7 +477,7 @@
             pltpu.VMEM((seqs, share, width), F32), pltpu.VMEM((seqs, 2 * share, wing), BF16),
             pltpu.VMEM((Q, width), F32), pltpu.VMEM((seqs, 2 * share, wing), BF16),
             pltpu.VMEM((8, Q), F32), pltpu.VMEM((seqs, 8, Q), F32),
-            dma((5,)), dma((5,)), dma((5,)), dma((PIECES,)), dma((PIECES,)),
+            dma((9,)), dma((5,)), dma((5,)), dma((PIECES,)), dma((PIECES,)),
             dma, dma, dma((2,)), dma((2,)), dma((2,)), dma((2,)),
         ],
         compiler_params=pltpu.CompilerParams(

time: 43.5 us -> 42.1 us (0.968)
  Pallas kernels: 41 us -> 39.6 us
    pallas_call x1, Pallas kernels: 41 us -> 39.6 us  [per_device(): pl.pallas_call(functools.partial(kernel, seqs, ways), out_shape=jax.Shape...]
where the time goes in v5:
time: 42.1 us; the launch traced here: 41.9 us
  Pallas kernels  39.6 us (94%)
  local copies, waits for them, and re-layouts  2.26 us (5%)
    pallas_call x1, Pallas kernels, per_device(): pl.pallas_call(functools.partial(kernel, seqs, ways), out_shape=jax.Shape...  39.6 us
    unnamed x1, local copies, waits for them, and re-layouts  2.26 us

profile of v5, /device:TPU:8, one launch (start us, length us, event | category | flops | bytes accessed | tf_op | source)
XLA Modules:
  0.0 41.9 jit_solution(2554594127343667977)
XLA Ops:
  0.0 39.6 %shard_map.82 = bf16[2048,256]{1,0:T(8,128)(2,1)} custom-call(bf16[2048,256]{1,0:T(8,128)(2,1)} %x_hbm.1, bf16[2048,256]{1,0:T(8,128)(2,1)} %bc_hbm.1, bf16[64,2048]{1,0:T(8,128)(2,1)} %dt_hbm.1, f32[4,4096]{1,0:T(4,128)} %wx_hbm.1, f32[4,256]{1,0:T(4,128)} %ws_hbm.1, f32[1,64]{1,0:T(1,128)} %bitcast.3, f32[1,64]{1,0:T(1,128)} %bitcast.4, f32[1,64]{1,0:T(1,128)} %bitcast.5), custom_call_target="tpu_custom_call" | custom-call | tf_op jit(solution)/shard_map/pallas_call | solution.py:458
  39.6 2.3 %copy.10 = bf16[2048,256]{1,0:T(8,128)(2,1)} copy(bf16[2048,256]{1,0:T(8,128)(2,1)} %shard_map.82) | data formatting | bytes 2097152

commit v6 on v5

--- a/solution.py
+++ b/solution.py
@@ -311,9 +311,14 @@
         span = buffer.at[pl.ds(0, count)]
         pltpu.make_async_copy(span, span, sem).wait()
 
+    def far_first(d):
+        moved = d + seqs // 4 - 1
+        moved = jnp.where(moved > seqs - 1, moved - (seqs - 1), moved)
+        return jnp.where(d == 0, 0, moved)
+
     def states_out(way):
         def go(d, _):
-            to_owner(way, d).start()
+            to_owner(way, far_first(d)).start()
             return 0
 
         lax.fori_loop(1, seqs, go, 0)
@@ -337,7 +342,7 @@
         lax.fori_loop(0, seqs, hop, jnp.zeros(got[way].shape[1:], F32))
 
         def go(d, _):
-            from_owner(way, d).start()
+            from_owner(way, far_first(d)).start()
             return 0
 
         lax.fori_loop(1 - way, seqs, go, 0)
@@ -400,12 +405,12 @@
     tot_f[...] = lax.fori_loop(0, chunks // 4, by(4, forward_total), jnp.zeros((Q, width), F32))
     states_out(0)
     lax.fori_loop(0, chunks // 4, by(4, step_maps), 0)
-    half = steps_of(own8, mate * HEADS + local, 0, er, fr)
-    exr[...] = chunk_decay(half, 0)
     everyone = dall.at[pl.ds(0, seqs - 1)]
     pltpu.make_async_copy(everyone, everyone, d_recv).wait()
     states_back(1)
     lax.fori_loop(6, PIECES, push, 0)
+    half = steps_of(own8, mate * HEADS + local, 0, er, fr)
+    exr[...] = chunk_decay(half, 0)
     halos[4].wait_recv()
 
     @pl.when(here == seqs - 1)

time: 42.1 us -> 42.1 us (level)
  no operation moved by 1% of the time
where the time goes in v6:
time: 42.1 us; the launch traced here: 41.9 us
  Pallas kernels  39.6 us (94%)
  local copies, waits for them, and re-layouts  2.26 us (5%)
    pallas_call x1, Pallas kernels, per_device(): pl.pallas_call(functools.partial(kernel, seqs, ways), out_shape=jax.Shape...  39.6 us
    unnamed x1, local copies, waits for them, and re-layouts  2.26 us

profile of v6, /device:TPU:8, one launch (start us, length us, event | category | flops | bytes accessed | tf_op | source)
XLA Modules:
  0.0 41.9 jit_solution(817744110362092368)
XLA Ops:
  0.0 39.6 %shard_map.82 = bf16[2048,256]{1,0:T(8,128)(2,1)} custom-call(bf16[2048,256]{1,0:T(8,128)(2,1)} %x_hbm.1, bf16[2048,256]{1,0:T(8,128)(2,1)} %bc_hbm.1, bf16[64,2048]{1,0:T(8,128)(2,1)} %dt_hbm.1, f32[4,4096]{1,0:T(4,128)} %wx_hbm.1, f32[4,256]{1,0:T(4,128)} %ws_hbm.1, f32[1,64]{1,0:T(1,128)} %bitcast.3, f32[1,64]{1,0:T(1,128)} %bitcast.4, f32[1,64]{1,0:T(1,128)} %bitcast.5), custom_call_target="tpu_custom_call" | custom-call | tf_op jit(solution)/shard_map/pallas_call | solution.py:463
  39.6 2.3 %copy.10 = bf16[2048,256]{1,0:T(8,128)(2,1)} copy(bf16[2048,256]{1,0:T(8,128)(2,1)} %shard_map.82) | data formatting | bytes 2097152

commit v7 on v5

--- a/solution.py
+++ b/solution.py
@@ -400,12 +400,12 @@
     tot_f[...] = lax.fori_loop(0, chunks // 4, by(4, forward_total), jnp.zeros((Q, width), F32))
     states_out(0)
     lax.fori_loop(0, chunks // 4, by(4, step_maps), 0)
-    half = steps_of(own8, mate * HEADS + local, 0, er, fr)
-    exr[...] = chunk_decay(half, 0)
     everyone = dall.at[pl.ds(0, seqs - 1)]
     pltpu.make_async_copy(everyone, everyone, d_recv).wait()
     states_back(1)
     lax.fori_loop(6, PIECES, push, 0)
+    half = steps_of(own8, mate * HEADS + local, 0, er, fr)
+    exr[...] = chunk_decay(half, 0)
     halos[4].wait_recv()
 
     @pl.when(here == seqs - 1)

time: 42.1 us -> 42.1 us (level)
  no operation moved by 1% of the time
where the time goes in v7:
time: 42.1 us; the launch traced here: 41.9 us
  Pallas kernels  39.6 us (94%)
  local copies, waits for them, and re-layouts  2.26 us (5%)
    pallas_call x1, Pallas kernels, per_device(): pl.pallas_call(functools.partial(kernel, seqs, ways), out_shape=jax.Shape...  39.6 us
    unnamed x1, local copies, waits for them, and re-layouts  2.26 us

profile of v7, /device:TPU:8, one launch (start us, length us, event | category | flops | bytes accessed | tf_op | source)
XLA Modules:
  0.0 41.9 jit_solution(3753319686676803366)
XLA Ops:
  0.0 39.6 %shard_map.82 = bf16[2048,256]{1,0:T(8,128)(2,1)} custom-call(bf16[2048,256]{1,0:T(8,128)(2,1)} %x_hbm.1, bf16[2048,256]{1,0:T(8,128)(2,1)} %bc_hbm.1, bf16[64,2048]{1,0:T(8,128)(2,1)} %dt_hbm.1, f32[4,4096]{1,0:T(4,128)} %wx_hbm.1, f32[4,256]{1,0:T(4,128)} %ws_hbm.1, f32[1,64]{1,0:T(1,128)} %bitcast.3, f32[1,64]{1,0:T(1,128)} %bitcast.4, f32[1,64]{1,0:T(1,128)} %bitcast.5), custom_call_target="tpu_custom_call" | custom-call | tf_op jit(solution)/shard_map/pallas_call | solution.py:458
  39.6 2.3 %copy.10 = bf16[2048,256]{1,0:T(8,128)(2,1)} copy(bf16[2048,256]{1,0:T(8,128)(2,1)} %shard_map.82) | data formatting | bytes 2097152
